TPU v7x, 32 devices: a whole 2x2x4 slice. The times are simulated.
32 devices in a mesh: dp: 16 (over z, x, core), tensor: 2 (over y).
Axes of the slice: x: 2, y: 2, z: 4, core: 2. Of those that a mesh axis runs over, the one named last changes fastest.
Arguments:
- tokens: bfloat16 [16384, 768], P(('dp', 'tensor')), may hold values from -6 to 6
- w_qkv: bfloat16 [3, 768, 768], P(None, None, 'tensor'), may hold values from -0.21875 to 0.21875
- attn_bias: float32 [2, 768], P(None, 'tensor'), may hold values from -3 to 3
- w_out: bfloat16 [768, 768], P('tensor'), may hold values from -0.875 to 0.875
- res_bias: float32 [2, 768], replicated, may hold values from -3 to 3
- w_in: bfloat16 [768, 3072], P(None, 'tensor'), may hold values from -0.21875 to 0.21875
- ffn_bias: float32 [3072], P('tensor'), may hold values from -3 to 3
- w_back: bfloat16 [3072, 768], P('tensor'), may hold values from -0.109375 to 0.109375
- norm_gains: float32 [2, 768], replicated, may hold values from 0.5 to 1.5
- norm_shifts: float32 [2, 768], replicated, may hold values from -3 to 3
- cotangent: bfloat16 [16384, 768], P(('dp', 'tensor')), may hold values from -6 to 6
- buckets: int32 [16], P('dp'), may hold values from 0 to 2, as said below
- lengths: int32 [16, 32], P('dp'), may hold values from 0 to 128, as said below
Outputs:
- output: bfloat16 [16384, 768], P(('dp', 'tensor'))
- grad_tokens: bfloat16 [16384, 768], P(('dp', 'tensor'))
- grad_qkv: float32 [3, 768, 768], P(None, None, 'tensor')
- grad_attn_bias: float32 [2, 768], P(None, 'tensor')
- grad_out: float32 [768, 768], P('tensor')
- grad_res_bias: float32 [2, 768], replicated
- grad_in: float32 [768, 3072], P(None, 'tensor')
- grad_ffn_bias: float32 [3072], P('tensor')
- grad_back: float32 [3072, 768], P('tensor')
- grad_norm_gains: float32 [2, 768], replicated
- grad_norm_shifts: float32 [2, 768], replicated
Inputs may be any that keep to these rules, and one draw needn't show every extreme that they name: `buckets`: every bucket value 0, 1 and 2 occurs in some row. `lengths`: A row of bucket b holds 1024 / (32 * 2**b) sentences; entry s is the length of the sentence that starts at token s * 32 * 2**b of the row, from 1 to 32 * 2**b, and one sentence of each row fills its slot; the later entries are 0.
All inputs are finite; a program needn't handle non-finite values.
Results may differ from a plain program's by a relative error of at most 0.015.
Values may be sent and summed in bfloat16 or wider, within the bound.
No kernel may reach another device: no remote copies, remote signals or barrier semaphores. Data moves between devices by JAX's collectives and lax.ppermute only.
A program may use at most 128 MiB of HBM per device.

v0:
```python
import functools
import math

import jax
import jax.numpy as jnp
import numpy as np
from jax import lax
from jax.experimental import pallas as pl
from jax.experimental.pallas import tpu as pltpu
from jax.sharding import PartitionSpec as P

HEAD_DIM = 64
ROW_LEN = 1024
TILE = 128
PAIR = 2 * HEAD_DIM
NEG = -1000000000.0
EPS = 1e-05
SCALE = HEAD_DIM ** (-0.5)
inv_root_two = 1.0 / math.sqrt(2.0)
inv_root_tau = 1.0 / math.sqrt(2.0 * math.pi)
f32 = jnp.float32
bf16 = jnp.bfloat16
MB = 1 << 20
LIMIT = 8
WIDE_LIMIT = 14
WIDE = {"feed_own", "feed_other", "back_grad", "in_grad_own", "in_grad_other", "qkv_grad"}

NN, NT, TN = ((1,), (0,)), ((1,), (1,)), ((0,), (0,))


def dot(a, b, dims=NN):
    return lax.dot_general(a, b, (dims, ((), ())), preferred_element_type=f32)


def sds(shape, dtype=bf16):
    return jax.ShapeDtypeStruct(shape, dtype)


def vmem():
    return pl.BlockSpec(memory_space=pltpu.VMEM)


def smem():
    return pl.BlockSpec(memory_space=pltpu.SMEM)


COST = pl.CostEstimate(flops=3 * 10**10, bytes_accessed=10**15, transcendentals=0)


LITTLE = pl.CostEstimate(flops=1, bytes_accessed=10**15, transcendentals=0)


def call(body, name, me, ins, outs, scratch=(), cost=COST):
    limit = WIDE_LIMIT if name in WIDE else LIMIT
    return pl.pallas_call(
        body,
        name=name,
        out_shape=outs,
        in_specs=[smem()] + [vmem()] * len(ins),
        out_specs=[vmem()] * len(outs),
        scratch_shapes=scratch,
        compiler_params=pltpu.CompilerParams(vmem_limit_bytes=limit * MB),
        cost_estimate=cost,
    )(me, *ins)


def packed(body, name, me, ins, outs):
    return pl.pallas_call(
        body,
        name=name,
        out_shape=outs,
        in_specs=[smem()] + [pl.BlockSpec(memory_space=pltpu.HBM)] * len(ins),
        out_specs=[vmem()] * len(outs),
        scratch_shapes=[pltpu.SemaphoreType.DMA((3,))],
        compiler_params=pltpu.CompilerParams(vmem_limit_bytes=LIMIT * MB),
        cost_estimate=COST,
    )(me, *[pltpu.with_memory_space_constraint(v, pltpu.HBM) for v in ins])


X, C, Z0, Z1, SIDE = range(5)


def rows_at(start, size):
    return pl.ds(pl.multiple_of(start, 16), size)


def head_lanes():
    return lax.broadcasted_iota(jnp.int32, (TILE, PAIR), 1) < HEAD_DIM


def both_heads(block):
    first = head_lanes()
    zero = jnp.zeros_like(block)
    return jnp.concatenate([jnp.where(first, block, zero), jnp.where(first, zero, block)], axis=0)


def side_by_side(stacked):
    return jnp.where(head_lanes(), stacked[:TILE], stacked[TILE:])


def project(x, w, bias, q, k, v):
    q[...] = (dot(x[...], w[0]) + bias[0]).astype(bf16)
    k[...] = dot(x[...], w[1]).astype(bf16)
    v[...] = (dot(x[...], w[2]) + bias[1]).astype(bf16)


def attention(mask, q, k, v, probs, ctx):
    tokens, width = q.shape
    pairs = width // PAIR
    for t in range(tokens // TILE):
        rows = pl.ds(t * TILE, TILE)
        bias = mask[t]
        bias = jnp.concatenate([bias, bias], axis=0)
        for p in range(pairs):
            lanes = pl.ds(p * PAIR, PAIR)
            queries = both_heads(q[rows, lanes] * jnp.asarray(SCALE, bf16))
            scores = dot(queries, k[rows, lanes], NT) + bias
            raised = jnp.exp(scores - jnp.max(scores, axis=-1, keepdims=True))
            prob = (raised / jnp.sum(raised, axis=-1, keepdims=True)).astype(bf16)
            probs[t * pairs + p] = prob
            ctx[rows, lanes] = side_by_side(dot(prob, v[rows, lanes])).astype(bf16)


def attend_own(me, x, w, bias, mask, q, k, v, probs, ctx, x_t):
    x_t[...] = x[...].T
    project(x, w, bias, q, k, v)
    attention(mask, q, k, v, probs, ctx)


def normed(z):
    centred = z - jnp.mean(z, axis=-1, keepdims=True)
    inv = lax.rsqrt(jnp.mean(centred * centred, axis=-1, keepdims=True) + EPS)
    return centred * inv, inv


def norm_back(grad_normed, n, inv):
    return inv * (
        grad_normed
        - jnp.mean(grad_normed, axis=-1, keepdims=True)
        - n * jnp.mean(grad_normed * n, axis=-1, keepdims=True)
    )


def attn_copies(piece, core, w_qkv, w_out, out, sems, first):
    rows = w_qkv.shape[1] // 8
    half = w_qkv.shape[2]
    out_rows = w_out.shape[0] // 8
    mine = w_out.at[rows_at((2 * piece + core) * out_rows, out_rows)]
    pairs = (
        (w_qkv.at[:, rows_at((2 * piece + core) * rows, rows), :], out.at[0:3]),
        (mine.at[:, 0:half], out.at[3, 0:out_rows]),
        (mine.at[:, half : 2 * half], out.at[3, out_rows : 2 * out_rows]),
    )
    return [pltpu.make_async_copy(a, b, sems.at[first + i]) for i, (a, b) in enumerate(pairs)]


def feed_copies(piece, core, w_in, w_back, out, sems, first):
    model, hidden = w_in.shape
    width, rows = hidden // 4, model // 2
    half = width // 2
    mine = w_back.at[rows_at(piece * width + core * half, half)]
    pairs = (
        (w_in.at[rows_at(core * rows, rows), pl.ds(pl.multiple_of(piece * width, 128), width)], out.at[0:rows]),
        (mine.at[:, 0:width], out.at[rows : rows + half]),
        (mine.at[:, width : 2 * width], out.at[rows + half : rows + 2 * half]),
    )
    return [pltpu.make_async_copy(a, b, sems.at[first + i]) for i, (a, b) in enumerate(pairs)]


def run_copies(copies):
    for copy in copies:
        copy.start()
    for copy in copies:
        copy.wait()


def pack_attn(opposite, me, w_qkv, w_out, out, sems):
    piece = 2 * me[X] + me[Z0]
    run_copies(attn_copies(3 - piece if opposite else piece, me[C], w_qkv, w_out, out, sems, 0))


def pack_feed(opposite, me, w_in, w_back, out, sems):
    piece = 2 * me[X] + me[Z0]
    run_copies(feed_copies(3 - piece if opposite else piece, me[C], w_in, w_back, out, sems, 0))


def pack_biases(me, attn_bias, ffn_bias, biases):
    width = biases.shape[2]
    for i in range(2):
        biases[i] = attn_bias[i : i + 1]
    for i in range(4):
        biases[2 + i] = ffn_bias[pl.ds(i * width, width)].reshape(1, width)


def attend_other(
    me, x, n0, n1_, n2, n3, c0, c1, c2, c3, bias, mask, ctx_own, wo_own, res_bias, gains, shifts,
    q, k, v, probs, ctx, w, wo_all, mid, mid_low, n1, r1,
):
    core = me[C]
    rows = n0.shape[1]
    half = wo_all.shape[1] // 2
    part = rows // 2
    for r, (near, across) in enumerate(((n0, c0), (n1_, c1), (n2, c2), (n3, c3))):
        piece = (2 * me[X] + me[Z0]) ^ r
        for c, block in ((core, near), (1 - core, across)):
            w[:, rows_at((2 * piece + c) * rows, rows), :] = block[0:3]
            wo_all[rows_at((2 * piece + c) * part, part), 0:half] = block[3, 0:part]
            wo_all[rows_at((2 * piece + c) * part, part), half : 2 * half] = block[3, part : 2 * part]
    project(x, w, bias, q, k, v)
    attention(mask, q, k, v, probs, ctx)
    attended = dot(ctx_own[...], wo_own[...]) + dot(ctx[...], wo_all[...]) + res_bias[0:1]
    n_one, inv = normed(x[...].astype(f32) + attended)
    n1[...] = n_one
    r1[...] = inv
    value = n_one * gains[0:1] + shifts[0:1]
    mid[...] = value
    mid_low[...] = value.astype(bf16)


def gelu_both(a):
    cdf = 0.5 * (1.0 + lax.erf(a * inv_root_two))
    return a * cdf, cdf + a * jnp.exp(-0.5 * a * a) * inv_root_tau


def feed_own(me, mid_low, w_in, bias, w_back, hidden, slope, total, mid_t):
    row = jnp.concatenate([bias[2 + i] for i in range(4)], axis=1)
    value, grad = gelu_both(dot(mid_low[...], w_in[...]) + row)
    value = value.astype(bf16)
    hidden[...] = value
    slope[...] = grad.astype(bf16)
    total[...] = dot(value, w_back[...])
    mid_t[...] = mid_low[...].T


def feed_other(
    me, mid_low, bias, f0, f1, f2, f3, c0, c1, c2, c3, total, mid, cotangent, res_bias, gains, shifts,
    hidden, slope, w_in, w_back, output, grad_two, fed, sums,
):
    core = me[C]
    model = w_in.shape[0]
    width = w_in.shape[1] // 4
    rows, half = model // 2, width // 2
    for r, (near, across) in enumerate(((f0, c0), (f1, c1), (f2, c2), (f3, c3))):
        for c, block in ((core, near), (1 - core, across)):
            w_in[rows_at(c * rows, rows), r * width : (r + 1) * width] = block[0:rows]
            to = rows_at(r * width + c * half, half)
            w_back[to, 0:width] = block[rows : rows + half]
            w_back[to, width : 2 * width] = block[rows + half : rows + 2 * half]
    row = jnp.concatenate([bias[2 + ((2 * me[X] + me[Z0]) ^ r)] for r in range(4)], axis=1)
    value, grad = gelu_both(dot(mid_low[...], w_in[...]) + row)
    value = value.astype(bf16)
    hidden[...] = value
    slope[...] = grad.astype(bf16)
    ffn = total[...] + res_bias[1:2] + dot(value, w_back[...])
    n2, inv = normed(mid[...] + ffn)
    output[...] = (n2 * gains[1:2] + shifts[1:2]).astype(bf16)
    g = cotangent[...].astype(f32)
    grad = norm_back(g * gains[1:2], n2, inv)
    grad_two[...] = grad
    low = grad.astype(bf16)
    fed[...] = low
    sums[0:1] = jnp.sum(low.astype(f32), axis=0, keepdims=True)
    sums[1:2] = jnp.sum(g * n2, axis=0, keepdims=True)
    sums[2:3] = jnp.sum(g, axis=0, keepdims=True)


def slot(core, own_or_other, rx, r0):
    first = core == 0
    return jnp.where(first, own_or_other, r0), jnp.where(first, rx, own_or_other), jnp.where(first, r0, rx)


def relative(me, h, quarter):
    if h:
        return quarter // 2, quarter % 2
    return me[X] ^ (quarter // 2), me[Z0] ^ (quarter % 2)


def back_grad(me, hid_own, hid_other, fed, away, keep, grads):
    core = me[C]
    width = hid_own.shape[1] // 4
    size = width // 4
    for h, hid in enumerate((hid_own, hid_other)):
        grads[h] = dot(hid[...], fed[...], TN).astype(bf16)
        for q in range(4):
            rx, r0 = relative(me, h, q)
            for c, out in ((1 - core, away), (core, keep)):
                for j in range(2):
                    out[*slot(c, h, rx, r0), j] = grads[h, rows_at(q * width + (2 * c + j) * size, size), :]


def in_grad(mid_t, fed, w_back, slope, w_in, bias_sums, place):
    pre = (dot(fed[...], w_back[...], NT) * slope[...].astype(f32)).astype(bf16)
    width = pre.shape[1] // 4
    sums = jnp.sum(pre.astype(f32), axis=0, keepdims=True)
    for q in range(4):
        bias_sums[place(q)] = sums[:, q * width : (q + 1) * width]
    return dot(mid_t[...], pre).astype(bf16), dot(pre, w_in[...], NT)


def in_grad_own(me, mid_t, fed, w_back, slope, w_in, grads, bias_sums, total):
    grads[...], total[...] = in_grad(mid_t, fed, w_back, slope, w_in, bias_sums, lambda q: q)


def in_grad_other(
    me, mid_t, fed, w_back, slope, w_in, grads_own, total_own, grad_two, n1, r1, gains,
    away, keep, bias_sums, grad_one, grad_att, sums, grads,
):
    core, here = me[C], 2 * me[X] + me[Z0]
    grads[...], part = in_grad(mid_t, fed, w_back, slope, w_in, bias_sums, lambda q: here ^ q)
    width = w_in.shape[1] // 4
    size = w_in.shape[0] // 4
    for h, source in ((0, grads_own), (1, grads)):
        for q in range(4):
            rx, r0 = relative(me, h, q)
            for c, out in ((1 - core, away), (core, keep)):
                for j in range(2):
                    out[*slot(c, h, rx, r0), j] = source[
                        rows_at((2 * c + j) * size, size), q * width : (q + 1) * width
                    ]
    grad_mid = grad_two[...] + total_own[...] + part
    n = n1[...]
    sums[1:2] = jnp.sum(grad_mid * n, axis=0, keepdims=True)
    sums[2:3] = jnp.sum(grad_mid, axis=0, keepdims=True)
    grad = norm_back(grad_mid * gains[0:1], n, r1[...])
    grad_one[...] = grad
    low = grad.astype(bf16)
    grad_att[...] = low
    sums[0:1] = jnp.sum(low.astype(f32), axis=0, keepdims=True)


def attend_back(me, grad_att, w_out, ctx, q, k, v, probs, grads, grad_out, gctx):
    half = grad_out.shape[2]
    gctx[...] = dot(grad_att[...], w_out[...], NT).astype(bf16)
    grad = dot(ctx[...], grad_att[...], TN).astype(bf16)
    grad_out[0] = grad[:, :half]
    grad_out[1] = grad[:, half:]
    tokens, width = q.shape
    pairs = width // PAIR
    for t in range(tokens // TILE):
        rows = pl.ds(t * TILE, TILE)
        for p in range(pairs):
            lanes = pl.ds(p * PAIR, PAIR)
            prob = probs[t * pairs + p]
            context = both_heads(gctx[rows, lanes])
            grads[rows, pl.ds(2 * width + p * PAIR, PAIR)] = dot(prob, context, TN).astype(bf16)
            grad_prob = dot(context, v[rows, lanes], NT)
            prob = prob.astype(f32)
            mean = jnp.sum(prob * grad_prob, axis=-1, keepdims=True)
            score = (prob * (grad_prob - mean)).astype(bf16)
            grads[rows, lanes] = (side_by_side(dot(score, k[rows, lanes])) * SCALE).astype(bf16)
            queries = both_heads(q[rows, lanes])
            grads[rows, pl.ds(width + p * PAIR, PAIR)] = (dot(score, queries, TN) * SCALE).astype(bf16)


def qkv_grad(
    me, x_t, own, own_out, oth, oth_out, sums_one, sums_two, ffn_own, ffn_other, away, keep, grads, small,
):
    mx, mc, m0 = me[X], me[C], me[Z0]
    half = keep.shape[5]
    size = half // 8
    small[...] = jnp.zeros_like(small)
    for h, g, out, ffn in ((0, own, own_out, ffn_own), (1, oth, oth_out, ffn_other)):
        grads[h] = dot(x_t[...], g[...]).astype(bf16)
        rows = [s[i : i + 1, j * half : (j + 1) * half] for s in (sums_one, sums_two) for i in range(3) for j in range(2)]
        rows += [ffn[i] for i in range(4)]
        rows += [
            jnp.sum(g[:, c * half : (c + 1) * half].astype(f32), axis=0, keepdims=True) for c in (0, 2)
        ]
        for i, row in enumerate(rows):
            small[h, i // 2, i % 2 : i % 2 + 1] = row
        for core, piece in ((1 - mc, away), (mc, keep)):
            for rx in range(2):
                for r0 in range(2):
                    place = 4 * core + 2 * (mx ^ rx) + (m0 ^ r0)
                    for j in range(2):
                        to = (*slot(core, h, rx, r0), j)
                        for c in range(3):
                            piece[*to, c * size : (c + 1) * size, :] = grads[
                                h, rows_at(size * (2 * place + j), size), c * half : (c + 1) * half
                            ]
                        piece[*to, 3 * size : 4 * size, :] = out[j, rows_at(size * place, size), :]
                        piece[*to, 4 * size : 4 * size + 16, :] = split(small[h, 2 * place + j])


def split(values):
    high = values.astype(bf16).astype(f32)
    rest = values - high
    middle = rest.astype(bf16).astype(f32)
    fill = jnp.zeros((10, values.shape[1]), f32)
    return jnp.concatenate([high, middle, rest - middle, fill], axis=0).astype(bf16)


def joined(rows):
    rows = rows.astype(f32)
    return rows[0:2] + rows[2:4] + rows[4:6]


def token_grad(me, grad_one, own, oth, w_own, w_other, out):
    total = grad_one[...]
    half = w_own.shape[2]
    for g, w in ((own, w_own), (oth, w_other)):
        for c in range(3):
            total += dot(g[:, c * half : (c + 1) * half], w[c], NT)
    out[...] = total.astype(bf16)


def place_rows(by_rows, me, b0, b1, b2, b3, out):
    size, width = b0.shape[2:]
    for place in range(4):
        rx, r0 = me[X] ^ (place // 2), me[Z0] ^ (place % 2)
        for c, blocks in ((0, (b0, b2)), (1, (b1, b3))):
            core = me[C] ^ c
            for last, block in enumerate(blocks):

                @pl.when(jnp.where(core == 0, rx, r0) == last)
                def _():
                    for j in range(2):
                        start = (2 * core + j) * size
                        start = pl.multiple_of(start + place * 4 * size if by_rows else start, 8)
                        lanes = slice(0, width) if by_rows else slice(place * width, (place + 1) * width)
                        out[pl.ds(start, size), lanes] = block[jnp.where(core == 0, r0, rx), j].astype(f32)


def place_attn(me, b0, b1, b2, b3, qkv, w_out, attn_bias, res_bias, ffn_bias, gains, shifts, small):
    half = b0.shape[3]
    size = half // 8
    for c, blocks in ((0, (b0, b2)), (1, (b1, b3))):
        core = me[C] ^ c
        for last, block in enumerate(blocks):
            for inner in range(2):
                rx, r0 = jnp.where(core == 0, last, inner), jnp.where(core == 0, inner, last)
                start = 4 * core + 2 * (me[X] ^ rx) + (me[Z0] ^ r0)
                for j in range(2):
                    rows = pl.ds(pl.multiple_of((2 * start + j) * size, 8), size)
                    for n in range(3):
                        qkv[n, rows, :] = block[inner, j, n * size : (n + 1) * size].astype(f32)
                    rows = pl.ds(pl.multiple_of(start * size, 8), size)
                    w_out[rows, j * half : (j + 1) * half] = block[inner, j, 3 * size : 4 * size].astype(f32)
                    small[2 * start + j] = joined(block[inner, j, 4 * size : 4 * size + 16])
    row = lambda i: small[i // 2, i % 2 : i % 2 + 1]
    for out, first in ((res_bias, 0), (gains, 2), (shifts, 4)):
        for i in range(2):
            for j in range(2):
                out[i : i + 1, j * half : (j + 1) * half] = row(first + 6 * i + j)
    for i in range(4):
        ffn_bias[pl.ds(i * half, half)] = row(12 + i).reshape(half)
    for i in range(2):
        attn_bias[i : i + 1] = row(16 + i)


def add_parts(places, small, me, *refs):
    *ins, out = refs
    lead = out.shape[:-2]
    for i in range(math.prod(lead)):
        at = tuple(int(v) for v in np.unravel_index(i, lead))
        total = ins[0][(*places[0], *at)].astype(f32)
        for place, part in zip(places[1:], ins[1:]):
            total += part[(*place, *at)].astype(f32)
        if small:
            n = out.shape[-2] - 16
            tails = [part[(*place, *at)][n:] for place, part in zip(places, ins)]
            out[(*at, slice(0, n))] = total[:n].astype(out.dtype)
            out[(*at, slice(n, n + 16))] = split(sum(joined(t) for t in tails))
        else:
            out[at] = total.astype(out.dtype)


def join(me, a, b, out):
    out[0] = a[...]
    out[1] = b[...]


def tick(me, x, out):
    out[...] = x[...]


def choose(me, a, b, out):
    @pl.when(me[C] == 0)
    def _():
        out[...] = a[...]

    @pl.when(me[C] == 1)
    def _():
        out[...] = b[...]


def mask_bias(bucket, length_row, side, count):
    width = jnp.where(bucket == 0, 32, jnp.where(bucket == 1, 64, 128)).astype(jnp.int32)
    place = side * count + jnp.arange(count, dtype=jnp.int32)
    slot = place // width
    inside = place - slot * width
    match = slot[:, None] == jnp.arange(length_row.shape[0], dtype=jnp.int32)[None, :]
    length = jnp.sum(jnp.where(match, length_row[None, :], 0), axis=1)
    slot, key_ok = slot.reshape(-1, TILE), (inside < length).reshape(-1, TILE)
    same = slot[:, :, None] == slot[:, None, :]
    return jnp.where(same & key_ok[:, None, :], 0.0, NEG).astype(f32)


ORDER = (
    "back", "in1", "B_S0", "in2", "ab1", "I_S0", "ab2", "qkv+B_p0", "B_S1", "A_S0", "I_S1", "B_S2",
    "tok", "B_S3", "I_S2", "A_S1", "B_A0", "A_S2", "I_S3", "A_S3+B_g0", "B_A1", "I_A0", "A_A0+B_gc",
    "I_A1", "A_A1", "B_P+I_gc", "I_P+A_gc", "A_P",
)
def per_device(
    dp_size, tokens, w_qkv, attn_bias, w_out, res_bias, w_in, ffn_bias, w_back,
    norm_gains, norm_shifts, cotangent, buckets, lengths,
):
    here = lax.axis_index("dp")
    side = lax.axis_index("tensor")
    n_bits = dp_size.bit_length() - 1
    assert 1 << n_bits == dp_size and n_bits >= 4

    def bit(b):
        return (here >> b) & 1

    me = jnp.stack([bit(1), bit(0), bit(2), bit(3), side]).astype(jnp.int32)

    def over_dp(value, b):
        return lax.ppermute(value, "dp", [(i, i ^ (1 << b)) for i in range(dp_size)])

    def over_tensor(value):
        return lax.ppermute(value, "tensor", [(0, 1), (1, 0)])

    y, x, z0, z1 = 1, 4, 8, 16
    reduce_steps = (y, z0), (x, y), (z0, x)
    gather_steps = (z0, x), (x, z0)

    def flip(value, partners):
        pairs = [(i, i ^ partners[(i >> 1) & 1]) for i in range(2 * dp_size)]
        return lax.ppermute(value, ("dp", "tensor"), pairs)

    n_tokens, model = tokens.shape
    half = w_qkv.shape[2]
    hidden_half = w_in.shape[1]
    quarter = hidden_half // 4
    n_units = n_tokens // TILE * (half // PAIR)

    def after(value, *others):
        return lax.optimization_barrier((value, *others))[0]

    clock = [me]
    waits = []

    def step(body, *inputs, wait=()):
        flat, tree = jax.tree.flatten(inputs)
        held = lax.optimization_barrier((*flat, clock[0], *jax.tree.leaves(wait), *waits))
        waits.clear()
        out = body(*jax.tree.unflatten(tree, held[: len(flat)]))
        clock[0] = jax.tree.leaves(out)[0]
        return out

    def kernel(body, name, ins, outs, scratch=(), wait=(), cost=COST):
        return step(lambda *a: call(body, name, me, a, outs, scratch=scratch, cost=cost), *ins, wait=wait)

    near_shape = sds((4, model // 8, half))
    feed_shape = sds((model, quarter))
    near, = packed(functools.partial(pack_attn, False), "pack_near", me, (w_qkv, w_out), [near_shape])
    near_y = over_tensor(near)
    clock[0] = near
    biases, = kernel(pack_biases, "pack_biases", (attn_bias, ffn_bias), [sds((6, 1, quarter), f32)])
    biases_other = over_tensor(biases)

    def pack(body, name, opposite, weights, shape, wait=()):
        out, = step(
            lambda *w: packed(functools.partial(body, opposite), name, me, w, [shape]), *weights, wait=wait
        )
        return over_tensor(out)

    feed_y = pack(pack_feed, "pack_feed", False, (w_in, w_back), feed_shape)
    near_z, near_x = over_dp(near_y, 2), over_dp(near_y, 1)
    mask = step(lambda b, l: mask_bias(b, l, side, n_tokens), buckets[0], lengths[0])

    act = sds((n_tokens, half))
    probs = sds((n_units, 2 * TILE, TILE))
    wide = sds((n_tokens, model), f32)
    column = sds((n_tokens, 1), f32)
    own_q, own_k, own_v, own_p, own_ctx, tokens_t = kernel(
        attend_own, "attend_own", (tokens, w_qkv, biases, mask),
        [act, act, act, probs, act, sds((model, n_tokens))], cost=LITTLE,
    )
    near_c = [over_dp(after(v, own_ctx), 0) for v in (near_y, near_z, near_x)]
    passed, = kernel(choose, "choose", (near_z, near_x), [near_shape])
    near_d = flip(passed, (x, z0))
    feed_z, feed_x = over_dp(feed_y, 2), over_dp(feed_y, 1)
    turn, = kernel(tick, "tick", (mask[0, :8],), [sds((8, TILE), f32)], wait=(feed_y, biases_other, *near_c))
    feed_d_y = pack(pack_feed, "pack_feed_d", True, (w_in, w_back), feed_shape)
    near_all = near_y, near_z, near_x, near_d
    near_c.append(over_dp(after(near_d, turn), 0))
    (oth_q, oth_k, oth_v, oth_p, oth_ctx, w_qkv_other, w_out_other, mid, mid_low, n1, r1) = kernel(
        attend_other, "attend_other",
        (tokens, *near_all, *near_c, biases_other, mask, own_ctx, w_out,
         res_bias, norm_gains, norm_shifts),
        [act, act, act, probs, act, sds(w_qkv.shape), sds(w_out.shape), wide, sds(tokens.shape), wide, column],
        cost=LITTLE,
    )

    hidden_own, slope_own, total_own, mid_t = kernel(
        feed_own, "feed_own", (mid_low, w_in, biases, w_back),
        [sds((n_tokens, hidden_half)), sds((n_tokens, hidden_half)), wide, sds((model, n_tokens))],
        wait=feed_y, cost=LITTLE,
    )
    feed_all = feed_y, feed_z, feed_x, feed_d_y
    feed_c = [over_dp(after(feed_y, mid_low), 0)] + [over_dp(after(v, total_own), 0) for v in feed_all[1:]]
    (hidden_other, slope_other, w_in_other, w_back_other, output, grad_two, fed, sums_two) = kernel(
        feed_other, "feed_other",
        (mid_low, biases_other, *feed_all, *feed_c, total_own, mid, cotangent,
         res_bias, norm_gains, norm_shifts),
        [sds((n_tokens, hidden_half)), sds((n_tokens, hidden_half)), sds(w_in.shape),
         sds(w_back.shape), sds(tokens.shape), wide, sds(tokens.shape), sds((3, model), f32)],
    )

    env = {}
    ops = {}
    flying = {}

    def sent(key, value):
        flying[key] = value
        return value

    def chain(name, finish):
        state = {}

        def add(name_of, parts, places, shape):
            body = functools.partial(add_parts, places, name == "A")
            return kernel(body, name_of, parts, [sds(shape)])[0]

        def reduce(i):
            def run():
                if i == 0:
                    state["parts"], state["places"] = list(env[name]), [(), ()]
                parts, places = state["parts"], state["places"]
                value = add("add_half", parts, [(*p, 1) for p in places], parts[0].shape[i + 1 :])
                parts.append(sent(f"{name}_p{i}", flip(value, reduce_steps[i])))
                state["places"] = [(*p, 0) for p in places] + [()]

            return run

        def exchange():
            value = add("add_all", state["parts"], state["places"], state["parts"][-1].shape)
            state["pair"] = value, sent(name + "_p3", flip(value, (z1, z1)))

        def gather(i):
            def run():
                pair = state["pair"]
                if i == 0:
                    value = add("add_two", pair, [(), ()], pair[0].shape)
                    for b in range(4, n_bits):
                        value = add("add_two", (value, over_dp(value, b)), [(), ()], value.shape)
                else:
                    value, = kernel(join, "join", pair, [sds((2, *pair[0].shape))])
                got = sent(f"{name}_g{i}", flip(value, gather_steps[i]))
                state["pair"] = value, got
                if i == 1:
                    value_c = sent(name + "_gc", over_dp(value, 0))
                    state["blocks"] = value, value_c, got
                    if name != "A":
                        core_end()

            return run

        for i in range(3):
            ops[f"{name}_S{i}"] = reduce(i)
        ops[name + "_S3"] = exchange
        for i in range(2):
            ops[f"{name}_A{i}"] = gather(i)

        def core_end():
            got = state["blocks"][2]
            state["blocks"] = *state["blocks"], over_dp(after(got, clock[0]) if name == "A" else got, 0)

        def place():
            if name == "A":
                core_end()
            env[name + "_result"] = finish(state["blocks"])

        ops[name + "_P"] = place

    sub = quarter // 4
    piece = sds((2, 2, 2, 2, sub, model))
    in_piece = sds((2, 2, 2, 2, model // 4, quarter))
    attn_piece = sds((2, 2, 2, 2, half // 2 + 16, half))
    raw_out = sds((2, half, model // 2))

    def back():
        away, keep = kernel(
            back_grad, "back_grad", (hidden_own, hidden_other, fed), [piece, piece],
            scratch=[pltpu.VMEM((2, hidden_half, model), bf16)],
        )
        env["B"] = keep, sent("B_c", over_dp(away, 0))

    def in_first():
        env["in_own"] = kernel(
            in_grad_own, "in_grad_own", (mid_t, fed, w_back, slope_own, w_in),
            [sds(w_in.shape), sds((4, 1, quarter), f32), wide],
        )

    def in_second():
        grads_own, bias_own, mid_own = env["in_own"]
        away, keep, bias_other, grad_one, grad_att, sums_one = kernel(
            in_grad_other, "in_grad_other",
            (mid_t, fed, w_back_other, slope_other, w_in_other, grads_own, mid_own, grad_two, n1, r1, norm_gains),
            [in_piece, in_piece, sds((4, 1, quarter), f32), wide, sds(tokens.shape), sds((3, model), f32)],
            scratch=[pltpu.VMEM(w_in.shape, bf16)],
        )
        env["I"] = keep, sent("I_c", over_dp(away, 0))
        env.update(bias_own=bias_own, bias_other=bias_other, grad_one=grad_one, grad_att=grad_att, sums_one=sums_one)

    def attn_back(w, ctx, q, k, v, p):
        return kernel(
            attend_back, "attend_back", (env["grad_att"], w, ctx, q, k, v, p),
            [sds((n_tokens, 3 * half)), raw_out],
            scratch=[pltpu.VMEM((n_tokens, half), bf16)],
        )

    def attn_first():
        env["own"] = attn_back(w_out, own_ctx, own_q, own_k, own_v, own_p)

    def attn_second():
        env["other"] = attn_back(w_out_other, oth_ctx, oth_q, oth_k, oth_v, oth_p)

    def qkv():
        away, keep = kernel(
            qkv_grad, "qkv_grad",
            (tokens_t, *env["own"], *env["other"], env["sums_one"], sums_two, env["bias_own"], env["bias_other"]),
            [attn_piece, attn_piece],
            scratch=[pltpu.VMEM((2, model, 3 * half), bf16), pltpu.VMEM((2, 16, 2, half), f32)],
        )
        env["A"] = keep, sent("A_c", over_dp(away, 0))

    def token():
        env["grad_tokens"], = kernel(
            token_grad, "token_grad", (env["grad_one"], env["own"][0], env["other"][0], w_qkv, w_qkv_other), [sds(tokens.shape)]
        )

    chain("B", lambda blocks: kernel(
        functools.partial(place_rows, True), "place_back", blocks, [sds(w_back.shape, f32)]
    ))
    chain("I", lambda blocks: kernel(
        functools.partial(place_rows, False), "place_in", blocks, [sds(w_in.shape, f32)]
    ))
    last_shapes = [w_qkv.shape, w_out.shape, (2, half), (2, model), (hidden_half,), (2, model), (2, model)]
    chain("A", lambda blocks: kernel(
        place_attn, "place_attn", blocks, [sds(shape, f32) for shape in last_shapes],
        scratch=[pltpu.VMEM((16, 2, half), f32)],
    ))
    ops.update({
        "back": back, "in1": in_first, "in2": in_second, "ab1": attn_first, "ab2": attn_second,
        "qkv": qkv, "tok": token,
    })
    for entry in ORDER:
        key, *ended = entry.split("+")
        waits.extend(flying.pop(p) for p in ended)
        ops.pop(key)()
    assert not ops
    grad_tokens = env["grad_tokens"]
    (grad_back,), (grad_in,) = env["B_result"], env["I_result"]
    grad_qkv, grad_out, grad_attn_bias, grad_res_bias, grad_ffn_bias, grad_gains, grad_shifts = env["A_result"]

    return (
        output,
        grad_tokens,
        grad_qkv,
        grad_attn_bias,
        grad_out,
        grad_res_bias,
        grad_in,
        grad_ffn_bias,
        grad_back,
        grad_gains,
        grad_shifts,
    )


def solution(mesh):
    dp_size = mesh.shape["dp"]
    placed = (
        P(("dp", "tensor"), None),
        P(None, None, "tensor"),
        P(None, "tensor"),
        P("tensor", None),
        P(),
        P(None, "tensor"),
        P("tensor"),
        P("tensor", None),
        P(),
        P(),
        P(("dp", "tensor"), None),
        P("dp"),
        P("dp", None),
    )
    return jax.shard_map(
        lambda *args: per_device(dp_size, *args),
        mesh=mesh,
        in_specs=placed,
        out_specs=(
            P(("dp", "tensor"), None),
            P(("dp", "tensor"), None),
            P(None, None, "tensor"),
            P(None, "tensor"),
            P("tensor", None),
            P(),
            P(None, "tensor"),
            P("tensor"),
            P("tensor", None),
            P(),
            P(),
        ),
        check_vma=False,
    )
```

profile of v0, /device:TPU:25, one launch (start us, length us, event | category | flops | bytes accessed | tf_op | source)
XLA Modules:
  0.0 191.6 jit_solution(2820536448516536473)
XLA Ops:
  12.7 3.0 %attend_own.1 = (bf16[512,384]{1,0:T(8,128)(2,1)S(1)}, bf16[512,384]{1,0:T(8,128)(2,1)S(1)}, bf16[512,384]{1,0:T(8,128)(2,1)S(1)}, bf16[12,256,128]{2,1,0:T(8,12...) custom-call(s32[5]{0:T(128)S(1)} %stack.23.me, bf16[512,768]{1,0:T(8,128)(2,1)S(1)} %copy-done, ...), custom_call_target="tpu_custom_call" | custom-call | flops 1 | bytes 999999986991104 | tf_op jit(solution)/shard_map/attend_own/pallas_call | solution.py:55
  15.7 3.3 %collective-permute-start.4 = (bf16[4,96,384]{2,1,0:T(8,128)(2,1)S(1)}, bf16[4,96,384]{2,1,0:T(8,128)(2,1)S(1)}, u32[]{:S(2)}, u32[]{:S(2)}) collective-permute-start(bf16[4,96,384]{2,1,0:T(8,128)(2,1)S(1)} %collective-permute-done.n0), channel_id=1, source_target_pairs={{0,2},{2,0},{4,6},{6,4},{8,10},{10,8},{12,14},{14,12},{16,18},{18,... | collective-permute-start | bytes 884744 | tf_op jit(solution)/shard_map/ppermute | solution.py:519
  28.8 4.5 %collective-permute-start.9 = (bf16[4,96,384]{2,1,0:T(8,128)(2,1)S(1)}, bf16[4,96,384]{2,1,0:T(8,128)(2,1)S(1)}, u32[]{:S(2)}, u32[]{:S(2)}) collective-permute-start(bf16[4,96,384]{2,1,0:T(8,128)(2,1)S(1)} %collective-permute-done.3.n3), channel_id=1, source_target_pairs={{0,2},{2,0},{4,6},{6,4},{8,10},{10,8},{12,14},{14,12},{16,18},{18,... | collective-permute-start | bytes 884744 | tf_op jit(solution)/shard_map/ppermute | solution.py:519
  34.5 4.6 %attend_other.1 = (bf16[512,384]{1,0:T(8,128)(2,1)S(1)}, bf16[512,384]{1,0:T(8,128)(2,1)S(1)}, bf16[512,384]{1,0:T(8,128)(2,1)S(1)}, bf16[12,256,128]{2,1,0:T(8,...) custom-call(s32[5]{0:T(128)S(1)} %stack.23.me, ...), custom_call_target="tpu_custom_call" | custom-call | flops 1 | bytes 999999986991104 | tf_op jit(solution)/shard_map/attend_other/pallas_call | solution.py:55
  39.5 3.6 %feed_own.1 = (bf16[512,1536]{1,0:T(8,128)(2,1)S(1)}, bf16[512,1536]{1,0:T(8,128)(2,1)S(1)}, f32[512,768]{1,0:T(8,128)S(1)}, bf16[768,512]{1,0:T(8,128)(2,1)S(1)}) custom-call(s32[5]{0:T(128)S(1)} %stack.23.me, bf16[512,768]{1,0:T(8,128)(2,1)S(1)} %get-tuple-element.287.mid_low, bf16[768,1536]{1,0:T(8,128)(2,1)S(1)} %copy-done.1, ...), custom_call_target="tpu_custom_call" | custom-call | flops 1 | bytes 999999986991104 | tf_op jit(solution)/shard_map/feed_own/pallas_call | solution.py:55
  46.9 6.0 %feed_other.1 = (bf16[512,1536]{1,0:T(8,128)(2,1)S(1)}, bf16[512,1536]{1,0:T(8,128)(2,1)S(1)}, bf16[768,1536]{1,0:T(8,128)(2,1)S(1)}, bf16[1536,768]{1,0:T(8,128...) custom-call(s32[5]{0:T(128)S(1)} %stack.23.me, ...), custom_call_target="tpu_custom_call" | custom-call | flops 30000001024 | bytes 999999986991104 | tf_op jit(solution)/shard_map/feed_other/pallas_call | solution.py:55
  52.9 4.0 %back_grad.1 = (bf16[2,2,2,2,96,768]{5,4,3,2,1,0:T(8,128)(2,1)S(1)}, bf16[2,2,2,2,96,768]{5,4,3,2,1,0:T(8,128)(2,1)S(1)}) custom-call(s32[5]{0:T(128)S(1)} %stack.23.me, bf16[512,1536]{1,0:T(8,128)(2,1)S(1)} %get-tuple-element.311.hid_own, bf16[512,1536]{1,0:T(8,128)(2,1)S(1)} %get-tuple-element.312.hid_other, bf16[512,768]{1,0:T(8,128)(2,1)S(1)} %get-tuple-element.329.fed), custom_call_target="tpu_custom_call" | custom-call | flops 30000001024 | bytes 999999986991104 | tf_op jit(solution)/shard_map/back_grad/pallas_call | solution.py:55
  57.1 4.4 %in_grad_own.1 = (bf16[768,1536]{1,0:T(8,128)(2,1)S(1)}, f32[4,1,384]{2,1,0:T(1,128)S(1)}, f32[512,768]{1,0:T(8,128)S(1)}) custom-call(s32[5]{0:T(128)S(1)} %stack.23.me, bf16[768,512]{1,0:T(8,128)(2,1)S(1)} %get-tuple-element.328.mid_t, bf16[512,768]{1,0:T(8,128)(2,1)S(1)} %get-tuple-element.329.fed, bf16[1536,768]{1,0:T(8,128)(2,1)S(1)} %copy-done.2, ...), custom_call_target="tpu_custom_call" | custom-call | flops 30000001024 | bytes 999999986991104 | tf_op jit(solution)/shard_map/in_grad_own/pallas_call | solution.py:55
  63.0 5.7 %in_grad_other.1 = (bf16[2,2,2,2,192,384]{5,4,3,2,1,0:T(8,128)(2,1)S(1)}, bf16[2,2,2,2,192,384]{5,4,3,2,1,0:T(8,128)(2,1)S(1)}, f32[4,1,384]{2,1,0:T(1,128)S(1)}...) custom-call(s32[5]{0:T(128)S(1)} %stack.23.me, ...), custom_call_target="tpu_custom_call" | custom-call | flops 30000001024 | bytes 999999986991104 | tf_op jit(solution)/shard_map/in_grad_other/pallas_call | solution.py:55
  70.6 5.2 %attend_back.2 = (bf16[512,1152]{1,0:T(8,128)(2,1)S(1)}, bf16[2,384,384]{2,1,0:T(8,128)(2,1)S(1)}) custom-call(s32[5]{0:T(128)S(1)} %stack.23.me, bf16[512,768]{1,0:T(8,128)(2,1)S(1)} %get-tuple-element.361.grad_att, bf16[384,768]{1,0:T(8,128)(2,1)S(1)} %copy-done.5, bf16[512,384]{1,0:T(8,128)(2,1)S(1)} %copy-done.7, ...), custom_call_target="tpu_custom_call" | custom-call | flops 30000001024 | bytes 999999986991104 | tf_op jit(solution)/shard_map/attend_back/pallas_call | solution.py:55
  76.9 5.2 %attend_back.3 = (bf16[512,1152]{1,0:T(8,128)(2,1)S(1)}, bf16[2,384,384]{2,1,0:T(8,128)(2,1)S(1)}) custom-call(s32[5]{0:T(128)S(1)} %stack.23.me, bf16[512,768]{1,0:T(8,128)(2,1)S(1)} %get-tuple-element.361.grad_att, bf16[384,768]{1,0:T(8,128)(2,1)S(1)} %get-tuple-element.362.w_out, bf16[512,384]{1,0:T(8,128)(2,1)S(1)} %get-tuple-element.363.ctx, ...), custom_call_target="tpu_custom_call" | custom-call | flops 30000001024 | bytes 999999986991104 | tf_op jit(solution)/shard_map/attend_back/pallas_call | solution.py:55
  82.2 3.3 %qkv_grad.1 = (bf16[2,2,2,2,208,384]{5,4,3,2,1,0:T(8,128)(2,1)S(1)}, bf16[2,2,2,2,208,384]{5,4,3,2,1,0:T(8,128)(2,1)S(1)}) custom-call(s32[5]{0:T(128)S(1)} %stack.23.me, bf16[768,512]{1,0:T(8,128)(2,1)S(1)} %get-tuple-element.377.x_t, bf16[512,1152]{1,0:T(8,128)(2,1)S(1)} %get-tuple-element.401.own, bf16[2,384,384]{2,1,0:T(8,128)(2,1)S(1)} %get-tuple-element.379.own_out, ...), custom_call_target="tpu_custom_call" | custom-call | flops 30000001024 | bytes 999999986991104 | tf_op jit(solution)/shard_map/qkv_grad/pallas_call | solution.py:55
  94.8 7.2 %collective-permute-done.20.refs_3_ = bf16[2,2,96,768]{3,2,1,0:T(8,128)(2,1)S(1)} collective-permute-done((bf16[2,2,96,768]{3,2,1,0:T(8,128)(2,1)S(1)}, bf16[2,2,96,768]{3,2,1,0:T(8,128)(2,1)S(1)}, u32[]{:S(2)}, u32[]{:S(2)}) %collective-permute-start.20) | collective-permute-done | bytes 589856 | tf_op jit(solution)/shard_map/ppermute | solution.py:530
  102.7 4.1 %token_grad.1 = bf16[512,768]{1,0:T(8,128)(2,1)} custom-call(s32[5]{0:T(128)S(1)} %stack.23.me, f32[512,768]{1,0:T(8,128)S(1)} %get-tuple-element.400.grad_one, bf16[512,1152]{1,0:T(8,128)(2,1)S(1)} %get-tuple-element.401.own, bf16[512,1152]{1,0:T(8,128)(2,1)S(1)} %get-tuple-element.402.oth, bf16[3,768,384]{2,1,0:T(8,128)(2,1)S(1)} %copy-done.3, ...), custom_call_target="tpu_custom_call" | custom-call | flops 30000001024 | bytes 999999986991104 | tf_op jit(solution)/shard_map/token_grad/pallas_call | solution.py:55
  110.7 3.9 %collective-permute-done.24.refs_3_ = bf16[2,2,192,384]{3,2,1,0:T(8,128)(2,1)S(1)} collective-permute-done((bf16[2,2,192,384]{3,2,1,0:T(8,128)(2,1)S(1)}, bf16[2,2,192,384]{3,2,1,0:T(8,128)(2,1)S(1)}, u32[]{:S(2)}, u32[]{:S(2)}) %collective-permute-start.24) | collective-permute-done | bytes 589856 | tf_op jit(solution)/shard_map/ppermute | solution.py:530
  117.1 7.9 %collective-permute-done.27.refs_1_ = bf16[2,96,768]{2,1,0:T(8,128)(2,1)S(1)} collective-permute-done((bf16[2,96,768]{2,1,0:T(8,128)(2,1)S(1)}, bf16[2,96,768]{2,1,0:T(8,128)(2,1)S(1)}, u32[]{:S(2)}, u32[]{:S(2)}) %collective-permute-start.27) | collective-permute-done | bytes 294944 | tf_op jit(solution)/shard_map/ppermute | solution.py:530
  130.5 3.6 %collective-permute-done.30.b = bf16[2,96,768]{2,1,0:T(8,128)(2,1)S(1)} collective-permute-done((bf16[2,96,768]{2,1,0:T(8,128)(2,1)S(1)}, bf16[2,96,768]{2,1,0:T(8,128)(2,1)S(1)}, u32[]{:S(2)}, u32[]{:S(2)}) %collective-permute-start.30) | collective-permute-done | bytes 294944 | tf_op jit(solution)/shard_map/ppermute | solution.py:530
  134.1 3.4 %collective-permute-done.28.refs_4_ = bf16[2,208,384]{2,1,0:T(8,128)(2,1)S(1)} collective-permute-done((bf16[2,208,384]{2,1,0:T(8,128)(2,1)S(1)}, bf16[2,208,384]{2,1,0:T(8,128)(2,1)S(1)}, u32[]{:S(2)}, u32[]{:S(2)}) %collective-permute-start.28) | collective-permute-done | bytes 319520 | tf_op jit(solution)/shard_map/ppermute | solution.py:530
  139.9 9.0 %collective-permute-start.33 = (bf16[2,2,96,768]{3,2,1,0:T(8,128)(2,1)S(1)}, bf16[2,2,96,768]{3,2,1,0:T(8,128)(2,1)S(1)}, u32[]{:S(2)}, u32[]{:S(2)}) collective-permute-start(bf16[2,2,96,768]{3,2,1,0:T(8,128)(2,1)S(1)} %join.3.b0), channel_id=1, source_target_pairs={{0,2},{2,0},{4,6},{6,4},{8,10},{10,8},{12,14},{14,12},{16,18},{18,... | collective-permute-start | bytes 1769480 | tf_op jit(solution)/shard_map/ppermute | solution.py:519
  151.3 6.1 %collective-permute-done.31.refs_1_ = bf16[2,208,384]{2,1,0:T(8,128)(2,1)S(1)} collective-permute-done((bf16[2,208,384]{2,1,0:T(8,128)(2,1)S(1)}, bf16[2,208,384]{2,1,0:T(8,128)(2,1)S(1)}, u32[]{:S(2)}, u32[]{:S(2)}) %collective-permute-start.31) | collective-permute-done | bytes 319520 | tf_op jit(solution)/shard_map/ppermute | solution.py:530
  161.7 8.0 %collective-permute-start.38 = (bf16[2,2,192,384]{3,2,1,0:T(8,128)(2,1)S(1)}, bf16[2,2,192,384]{3,2,1,0:T(8,128)(2,1)S(1)}, u32[]{:S(2)}, u32[]{:S(2)}) collective-permute-start(bf16[2,2,192,384]{3,2,1,0:T(8,128)(2,1)S(1)} %join.4.b0), channel_id=1, source_target_pairs={{0,2},{2,0},{4,6},{6,4},{8,10},{10,8},{12,14},{14,12},{16,18},{18,... | collective-permute-start | bytes 1769480 | tf_op jit(solution)/shard_map/ppermute | solution.py:519
  170.5 6.1 %collective-permute-start.36 = (bf16[2,2,208,384]{3,2,1,0:T(8,128)(2,1)S(1)}, bf16[2,2,208,384]{3,2,1,0:T(8,128)(2,1)S(1)}, u32[]{:S(2)}, u32[]{:S(2)}) collective-permute-start(bf16[2,2,208,384]{3,2,1,0:T(8,128)(2,1)S(1)} %join.5.b0), channel_id=1, source_target_pairs={{0,2},{2,0},{4,6},{6,4},{8,10},{10,8},{12,14},{14,12},{16,18},{18,... | collective-permute-start | bytes 1916936 | tf_op jit(solution)/shard_map/ppermute | solution.py:519
  179.5 3.2 %place_back.1 = f32[1536,768]{1,0:T(8,128)} custom-call(s32[5]{0:T(128)S(1)} %stack.23.me, bf16[2,2,96,768]{3,2,1,0:T(8,128)(2,1)S(1)} %join.3.b0, bf16[2,2,96,768]{3,2,1,0:T(8,128)(2,1)S(1)} %collective-permute-done.33.b1, bf16[2,2,96,768]{3,2,1,0:T(8,128)(2,1)S(1)} %collective-permute-done.41.b2, bf16[2,2,96,768]{3,2,1,0:T(8,128)(2,1)S(1)} %collective-permute-done.42.b3), custom_call_target="tpu_custom_call" | custom-call | flops 30000001024 | bytes 999999986991104 | tf_op jit(solution)/shard_map/place_back/pallas_call | solution.py:55
  182.7 3.2 %place_in.1 = f32[768,1536]{1,0:T(8,128)} custom-call(s32[5]{0:T(128)S(1)} %stack.23.me, bf16[2,2,192,384]{3,2,1,0:T(8,128)(2,1)S(1)} %join.4.b0, bf16[2,2,192,384]{3,2,1,0:T(8,128)(2,1)S(1)} %collective-permute-done.38.b1, bf16[2,2,192,384]{3,2,1,0:T(8,128)(2,1)S(1)} %collective-permute-done.39.b2, bf16[2,2,192,384]{3,2,1,0:T(8,128)(2,1)S(1)} %collective-permute-done.40.b3), custom_call_target="tpu_custom_call" | custom-call | flops 30000001024 | bytes 999999986991104 | tf_op jit(solution)/shard_map/place_in/pallas_call | solution.py:55
  (149 shorter events, 71.2 us)
Async XLA Ops:
  4.9 18.0 %collective-permute-start.8 = (f32[6,1,384]{2,1,0:T(1,128)S(1)}, f32[6,1,384]{2,1,0:T(1,128)S(1)}, u32[]{:S(2)}, u32[]{:S(2)}) collective-permute-start(f32[6,1,384]{2,1,0:T(1,128)S(1)} %pack_biases.1.bias), channel_id=1, source_target_pairs={{0,1},{1,0},{2,3},{3,2},{4,5},{5,4},{6,7},{7,6},{8,9},{9,8},{10,11... | collective-permute-start | bytes 27656 | tf_op jit(solution)/shard_map/ppermute | solution.py:522
  7.6 16.3 %collective-permute-start.7 = (bf16[768,384]{1,0:T(8,128)(2,1)}, bf16[768,384]{1,0:T(8,128)(2,1)S(1)}, u32[]{:S(2)}, u32[]{:S(2)}) collective-permute-start(bf16[768,384]{1,0:T(8,128)(2,1)} %pack_feed.1), channel_id=1, source_target_pairs={{0,1},{1,0},{2,3},{3,2},{4,5},{5,4},{6,7},{7,6},{8,9},{9,8},{10,11... | collective-permute-start | bytes 1769480 | tf_op jit(solution)/shard_map/ppermute | solution.py:522
  15.7 9.5 %collective-permute-start.4 = (bf16[4,96,384]{2,1,0:T(8,128)(2,1)S(1)}, bf16[4,96,384]{2,1,0:T(8,128)(2,1)S(1)}, u32[]{:S(2)}, u32[]{:S(2)}) collective-permute-start(bf16[4,96,384]{2,1,0:T(8,128)(2,1)S(1)} %collective-permute-done.n0), channel_id=1, source_target_pairs={{0,2},{2,0},{4,6},{6,4},{8,10},{10,8},{12,14},{14,12},{16,18},{18,... | collective-permute-start | bytes 884744 | tf_op jit(solution)/shard_map/ppermute | solution.py:519
  24.0 19.2 %collective-permute-start.11 = (bf16[768,384]{1,0:T(8,128)(2,1)S(1)}, bf16[768,384]{1,0:T(8,128)(2,1)S(1)}, u32[]{:S(2)}, u32[]{:S(2)}) collective-permute-start(bf16[768,384]{1,0:T(8,128)(2,1)S(1)} %collective-permute-done.7.f0), channel_id=1, source_target_pairs={{0,4},{2,6},{4,0},{6,2},{8,12},{10,14},{12,8},{14,10},{16,20},{18,... | collective-permute-start | bytes 1769480 | tf_op jit(solution)/shard_map/ppermute | solution.py:519
  25.2 18.0 %collective-permute-start.10 = (bf16[768,384]{1,0:T(8,128)(2,1)S(1)}, bf16[768,384]{1,0:T(8,128)(2,1)S(1)}, u32[]{:S(2)}, u32[]{:S(2)}) collective-permute-start(bf16[768,384]{1,0:T(8,128)(2,1)S(1)} %collective-permute-done.7.f0), channel_id=1, source_target_pairs={{0,8},{2,10},{4,12},{6,14},{8,0},{10,2},{12,4},{14,6},{16,24},{18,... | collective-permute-start | bytes 1769480 | tf_op jit(solution)/shard_map/ppermute | solution.py:519
  27.2 16.6 %collective-permute-start.12 = (bf16[768,384]{1,0:T(8,128)(2,1)S(1)}, bf16[768,384]{1,0:T(8,128)(2,1)S(1)}, u32[]{:S(2)}, u32[]{:S(2)}) collective-permute-start(bf16[768,384]{1,0:T(8,128)(2,1)S(1)} %pack_feed_d.1), channel_id=1, source_target_pairs={{0,1},{1,0},{2,3},{3,2},{4,5},{5,4},{6,7},{7,6},{8,9},{9,8},{10,11... | collective-permute-start | bytes 1769480 | tf_op jit(solution)/shard_map/ppermute | solution.py:522
  63.0 19.1 %collective-permute-start.19 = (bf16[2,2,2,96,768]{4,3,2,1,0:T(8,128)(2,1)S(1)}, bf16[2,2,2,96,768]{4,3,2,1,0:T(8,128)(2,1)S(1)}, u32[]{:S(2)}, u32[]{:S(2)}) collective-permute-start(bf16[2,2,2,96,768]{4,3,2,1,0:T(8,128)(2,1)S(1)} %add_half.9), channel_id=1, source_target_pairs={{0,1},{1,0},{2,10},{3,11},{4,5},{5,4},{6,14},{7,15},{8,9},{9,8},{1... | collective-permute-start | bytes 3538952 | tf_op jit(solution)/shard_map/ppermute | solution.py:530
  76.8 16.9 %collective-permute-start.21 = (bf16[2,2,2,192,384]{4,3,2,1,0:T(8,128)(2,1)S(1)}, bf16[2,2,2,192,384]{4,3,2,1,0:T(8,128)(2,1)S(1)}, u32[]{:S(2)}, u32[]{:S(2)}) collective-permute-start(bf16[2,2,2,192,384]{4,3,2,1,0:T(8,128)(2,1)S(1)} %add_half.10), channel_id=1, source_target_pairs={{0,1},{1,0},{2,10},{3,11},{4,5},{5,4},{6,14},{7,15},{8,9},{9,8},{1... | collective-permute-start | bytes 3538952 | tf_op jit(solution)/shard_map/ppermute | solution.py:530
  86.8 15.2 %collective-permute-start.20 = (bf16[2,2,96,768]{3,2,1,0:T(8,128)(2,1)S(1)}, bf16[2,2,96,768]{3,2,1,0:T(8,128)(2,1)S(1)}, u32[]{:S(2)}, u32[]{:S(2)}) collective-permute-start(bf16[2,2,96,768]{3,2,1,0:T(8,128)(2,1)S(1)} %add_half.11), channel_id=1, source_target_pairs={{0,4},{1,5},{2,3},{3,2},{4,0},{5,1},{6,7},{7,6},{8,12},{9,13},{10,... | collective-permute-start | bytes 1769480 | tf_op jit(solution)/shard_map/ppermute | solution.py:530
  92.4 22.9 %collective-permute-start.23 = (bf16[2,2,2,208,384]{4,3,2,1,0:T(8,128)(2,1)}, bf16[2,2,2,208,384]{4,3,2,1,0:T(8,128)(2,1)}, u32[]{:S(2)}, u32[]{:S(2)}) collective-permute-start(bf16[2,2,2,208,384]{4,3,2,1,0:T(8,128)(2,1)} %add_half.12), channel_id=1, source_target_pairs={{0,1},{1,0},{2,10},{3,11},{4,5},{5,4},{6,14},{7,15},{8,9},{9,8},{1... | collective-permute-start | bytes 3833864 | tf_op jit(solution)/shard_map/ppermute | solution.py:530
  94.5 20.1 %collective-permute-start.24 = (bf16[2,2,192,384]{3,2,1,0:T(8,128)(2,1)S(1)}, bf16[2,2,192,384]{3,2,1,0:T(8,128)(2,1)S(1)}, u32[]{:S(2)}, u32[]{:S(2)}) collective-permute-start(bf16[2,2,192,384]{3,2,1,0:T(8,128)(2,1)S(1)} %add_half.13), channel_id=1, source_target_pairs={{0,4},{1,5},{2,3},{3,2},{4,0},{5,1},{6,7},{7,6},{8,12},{9,13},{10,... | collective-permute-start | bytes 1769480 | tf_op jit(solution)/shard_map/ppermute | solution.py:530
  110.6 14.5 %collective-permute-start.27 = (bf16[2,96,768]{2,1,0:T(8,128)(2,1)S(1)}, bf16[2,96,768]{2,1,0:T(8,128)(2,1)S(1)}, u32[]{:S(2)}, u32[]{:S(2)}) collective-permute-start(bf16[2,96,768]{2,1,0:T(8,128)(2,1)S(1)} %add_all.3.refs_0_), channel_id=1, source_target_pairs={{0,16},{1,17},{2,18},{3,19},{4,20},{5,21},{6,22},{7,23},{8,24},{9,... | collective-permute-start | bytes 884744 | tf_op jit(solution)/shard_map/ppermute | solution.py:530
  115.3 14.4 %collective-permute-start.29 = (bf16[2,192,384]{2,1,0:T(8,128)(2,1)S(1)}, bf16[2,192,384]{2,1,0:T(8,128)(2,1)S(1)}, u32[]{:S(2)}, u32[]{:S(2)}) collective-permute-start(bf16[2,192,384]{2,1,0:T(8,128)(2,1)S(1)} %add_half.15), channel_id=1, source_target_pairs={{0,8},{1,9},{2,6},{3,7},{4,12},{5,13},{6,2},{7,3},{8,0},{9,1},{10,... | collective-permute-start | bytes 884744 | tf_op jit(solution)/shard_map/ppermute | solution.py:530
  117.0 9.6 %collective-permute-start.26 = (bf16[2,2,208,384]{3,2,1,0:T(8,128)(2,1)S(1)}, bf16[2,2,208,384]{3,2,1,0:T(8,128)(2,1)S(1)}, u32[]{:S(2)}, u32[]{:S(2)}) collective-permute-start(bf16[2,2,208,384]{3,2,1,0:T(8,128)(2,1)S(1)} %add_half.16), channel_id=1, source_target_pairs={{0,4},{1,5},{2,3},{3,2},{4,0},{5,1},{6,7},{7,6},{8,12},{9,13},{10,... | collective-permute-start | bytes 1916936 | tf_op jit(solution)/shard_map/ppermute | solution.py:530
  130.4 18.6 %collective-permute-start.32 = (bf16[2,192,384]{2,1,0:T(8,128)(2,1)S(1)}, bf16[2,192,384]{2,1,0:T(8,128)(2,1)S(1)}, u32[]{:S(2)}, u32[]{:S(2)}) collective-permute-start(bf16[2,192,384]{2,1,0:T(8,128)(2,1)S(1)} %add_all.4.refs_0_), channel_id=1, source_target_pairs={{0,16},{1,17},{2,18},{3,19},{4,20},{5,21},{6,22},{7,23},{8,24},{9,... | collective-permute-start | bytes 884744 | tf_op jit(solution)/shard_map/ppermute | solution.py:530
  139.1 18.4 %collective-permute-start.31 = (bf16[2,208,384]{2,1,0:T(8,128)(2,1)S(1)}, bf16[2,208,384]{2,1,0:T(8,128)(2,1)S(1)}, u32[]{:S(2)}, u32[]{:S(2)}) collective-permute-start(bf16[2,208,384]{2,1,0:T(8,128)(2,1)S(1)} %add_all.5.refs_0_), channel_id=1, source_target_pairs={{0,16},{1,17},{2,18},{3,19},{4,20},{5,21},{6,22},{7,23},{8,24},{9,... | collective-permute-start | bytes 958472 | tf_op jit(solution)/shard_map/ppermute | solution.py:530
  139.8 29.9 %collective-permute-start.41 = (bf16[2,2,96,768]{3,2,1,0:T(8,128)(2,1)S(1)}, bf16[2,2,96,768]{3,2,1,0:T(8,128)(2,1)S(1)}, u32[]{:S(2)}, u32[]{:S(2)}) collective-permute-start(bf16[2,2,96,768]{3,2,1,0:T(8,128)(2,1)S(1)} %join.3.b0), channel_id=1, source_target_pairs={{0,4},{1,5},{2,10},{3,11},{4,0},{5,1},{6,14},{7,15},{8,12},{9,13},... | collective-permute-start | bytes 1769480 | tf_op jit(solution)/shard_map/ppermute | solution.py:530
  139.9 17.5 %collective-permute-start.33 = (bf16[2,2,96,768]{3,2,1,0:T(8,128)(2,1)S(1)}, bf16[2,2,96,768]{3,2,1,0:T(8,128)(2,1)S(1)}, u32[]{:S(2)}, u32[]{:S(2)}) collective-permute-start(bf16[2,2,96,768]{3,2,1,0:T(8,128)(2,1)S(1)} %join.3.b0), channel_id=1, source_target_pairs={{0,2},{2,0},{4,6},{6,4},{8,10},{10,8},{12,14},{14,12},{16,18},{18,... | collective-permute-start | bytes 1769480 | tf_op jit(solution)/shard_map/ppermute | solution.py:519
  149.6 10.3 %collective-permute-start.35 = (bf16[2,192,384]{2,1,0:T(8,128)(2,1)S(1)}, bf16[2,192,384]{2,1,0:T(8,128)(2,1)S(1)}, u32[]{:S(2)}, u32[]{:S(2)}) collective-permute-start(bf16[2,192,384]{2,1,0:T(8,128)(2,1)S(1)} %add_two.4.a), channel_id=1, source_target_pairs={{0,8},{1,9},{2,6},{3,7},{4,12},{5,13},{6,2},{7,3},{8,0},{9,1},{10,... | collective-permute-start | bytes 884744 | tf_op jit(solution)/shard_map/ppermute | solution.py:530
  158.1 11.7 %collective-permute-start.34 = (bf16[2,208,384]{2,1,0:T(8,128)(2,1)S(1)}, bf16[2,208,384]{2,1,0:T(8,128)(2,1)S(1)}, u32[]{:S(2)}, u32[]{:S(2)}) collective-permute-start(bf16[2,208,384]{2,1,0:T(8,128)(2,1)S(1)} %add_two.5.a), channel_id=1, source_target_pairs={{0,8},{1,9},{2,6},{3,7},{4,12},{5,13},{6,2},{7,3},{8,0},{9,1},{10,... | collective-permute-start | bytes 958472 | tf_op jit(solution)/shard_map/ppermute | solution.py:530
  160.5 16.1 %collective-permute-start.39 = (bf16[2,2,192,384]{3,2,1,0:T(8,128)(2,1)S(1)}, bf16[2,2,192,384]{3,2,1,0:T(8,128)(2,1)S(1)}, u32[]{:S(2)}, u32[]{:S(2)}) collective-permute-start(bf16[2,2,192,384]{3,2,1,0:T(8,128)(2,1)S(1)} %join.4.b0), channel_id=1, source_target_pairs={{0,4},{1,5},{2,10},{3,11},{4,0},{5,1},{6,14},{7,15},{8,12},{9,13},... | collective-permute-start | bytes 1769480 | tf_op jit(solution)/shard_map/ppermute | solution.py:530
  161.7 14.9 %collective-permute-start.38 = (bf16[2,2,192,384]{3,2,1,0:T(8,128)(2,1)S(1)}, bf16[2,2,192,384]{3,2,1,0:T(8,128)(2,1)S(1)}, u32[]{:S(2)}, u32[]{:S(2)}) collective-permute-start(bf16[2,2,192,384]{3,2,1,0:T(8,128)(2,1)S(1)} %join.4.b0), channel_id=1, source_target_pairs={{0,2},{2,0},{4,6},{6,4},{8,10},{10,8},{12,14},{14,12},{16,18},{18,... | collective-permute-start | bytes 1769480 | tf_op jit(solution)/shard_map/ppermute | solution.py:519
  170.4 15.5 %collective-permute-start.37 = (bf16[2,2,208,384]{3,2,1,0:T(8,128)(2,1)S(1)}, bf16[2,2,208,384]{3,2,1,0:T(8,128)(2,1)S(1)}, u32[]{:S(2)}, u32[]{:S(2)}) collective-permute-start(bf16[2,2,208,384]{3,2,1,0:T(8,128)(2,1)S(1)} %join.5.b0), channel_id=1, source_target_pairs={{0,4},{1,5},{2,10},{3,11},{4,0},{5,1},{6,14},{7,15},{8,12},{9,13},... | collective-permute-start | bytes 1916936 | tf_op jit(solution)/shard_map/ppermute | solution.py:530
  170.5 12.2 %collective-permute-start.36 = (bf16[2,2,208,384]{3,2,1,0:T(8,128)(2,1)S(1)}, bf16[2,2,208,384]{3,2,1,0:T(8,128)(2,1)S(1)}, u32[]{:S(2)}, u32[]{:S(2)}) collective-permute-start(bf16[2,2,208,384]{3,2,1,0:T(8,128)(2,1)S(1)} %join.5.b0), channel_id=1, source_target_pairs={{0,2},{2,0},{4,6},{6,4},{8,10},{10,8},{12,14},{14,12},{16,18},{18,... | collective-permute-start | bytes 1916936 | tf_op jit(solution)/shard_map/ppermute | solution.py:519
  (41 other events, 277.6 us)
where the time goes:
time: 195 us; the launch traced here: 192 us
  Pallas kernels  82.5 us (42%)
  starting transfers between devices  59.4 us (30%)
  waiting for transfers between devices  46.3 us (24%)
  between operations  2 us (1%)
    pallas_call x34, Pallas kernels, call(): pl.pallas_call(body, name=name, out_shape=outs, in_specs=[smem()] + [vmem...  76 us
    ppermute x21, starting transfers between devices, over_dp(): return lax.ppermute(value, 'dp', [(i, i ^ 1 << b) for i in range(dp_size)])  44.6 us
    ppermute x19, waiting for transfers between devices, flip(): return lax.ppermute(value, ('dp', 'tensor'), pairs)  36.1 us
    ppermute x19, starting transfers between devices, flip(): return lax.ppermute(value, ('dp', 'tensor'), pairs)  10.6 us
    ppermute x21, waiting for transfers between devices, over_dp(): return lax.ppermute(value, 'dp', [(i, i ^ 1 << b) for i in range(dp_size)])  8.36 us
    pallas_call x3, Pallas kernels, packed(): pl.pallas_call(body, name=name, out_shape=outs, in_specs=[smem()] + [pl.B...  6.49 us
    ppermute x4, starting transfers between devices, over_tensor(): return lax.ppermute(value, 'tensor', [(0, 1), (1, 0)])  4.21 us
  transfers between devices with their start and end apart: 44, of which 17 were waited for; matrix products, arithmetic and copies ran while one was open for 0% of the time, Pallas kernels for 35%

commit v1 on v0

--- a/solution.py
+++ b/solution.py
@@ -21,7 +21,7 @@
 f32 = jnp.float32
 bf16 = jnp.bfloat16
 MB = 1 << 20
-LIMIT = 8
+LIMIT = 12
 WIDE_LIMIT = 14
 WIDE = {"feed_own", "feed_other", "back_grad", "in_grad_own", "in_grad_other", "qkv_grad"}
 
@@ -497,9 +497,9 @@
 
 
 ORDER = (
-    "back", "in1", "B_S0", "in2", "ab1", "I_S0", "ab2", "qkv+B_p0", "B_S1", "A_S0", "I_S1", "B_S2",
-    "tok", "B_S3", "I_S2", "A_S1", "B_A0", "A_S2", "I_S3", "A_S3+B_g0", "B_A1", "I_A0", "A_A0+B_gc",
-    "I_A1", "A_A1", "B_P+I_gc", "I_P+A_gc", "A_P",
+    "back", "in1", "B_S0", "in2", "ab2", "I_S0", "ab1+B_p0", "qkv", "B_S1", "A_S0", "B_S2+I_p0",
+    "tok", "I_S1", "B_S3", "A_S1", "I_S2", "A_S2", "B_A0", "I_S3", "A_S3", "I_A0+B_g0", "B_A1",
+    "A_A0", "I_A1+B_gc", "A_A1", "B_P+I_gc", "I_P+A_gc", "A_P",
 )
 def per_device(
     dp_size, tokens, w_qkv, attn_bias, w_out, res_bias, w_in, ffn_bias, w_back,

time: 195 us -> 193 us (0.990)
  the two profiles are of different devices: /device:TPU:25 before, /device:TPU:17 now
where the time goes in v1:
time: 193 us; the launch traced here: 190 us
  Pallas kernels  79.2 us (41%)
  starting transfers between devices  70.6 us (37%)
  waiting for transfers between devices  36.5 us (19%)
  between operations  2.01 us (1%)
    pallas_call x34, Pallas kernels, call(): pl.pallas_call(body, name=name, out_shape=outs, in_specs=[smem()] + [vmem...  72.7 us
    ppermute x21, starting transfers between devices, over_dp(): return lax.ppermute(value, 'dp', [(i, i ^ 1 << b) for i in range(dp_size)])  45 us
    ppermute x19, waiting for transfers between devices, flip(): return lax.ppermute(value, ('dp', 'tensor'), pairs)  27.2 us
    ppermute x19, starting transfers between devices, flip(): return lax.ppermute(value, ('dp', 'tensor'), pairs)  21.3 us
    ppermute x21, waiting for transfers between devices, over_dp(): return lax.ppermute(value, 'dp', [(i, i ^ 1 << b) for i in range(dp_size)])  8.24 us
    pallas_call x3, Pallas kernels, packed(): pl.pallas_call(body, name=name, out_shape=outs, in_specs=[smem()] + [pl.B...  6.49 us
    ppermute x4, starting transfers between devices, over_tensor(): return lax.ppermute(value, 'tensor', [(0, 1), (1, 0)])  4.21 us
  transfers between devices with their start and end apart: 44, of which 16 were waited for; matrix products, arithmetic and copies ran while one was open for 0% of the time, Pallas kernels for 33%

profile of v1, /device:TPU:17, one launch (start us, length us, event | category | flops | bytes accessed | tf_op | source)
XLA Modules:
  0.0 190.0 jit_solution(7263735626569805033)
XLA Ops:
  16.8 3.3 %collective-permute-start.4 = (bf16[4,96,384]{2,1,0:T(8,128)(2,1)S(1)}, bf16[4,96,384]{2,1,0:T(8,128)(2,1)S(1)}, u32[]{:S(2)}, u32[]{:S(2)}) collective-permute-start(bf16[4,96,384]{2,1,0:T(8,128)(2,1)S(1)} %collective-permute-done.n0), channel_id=1, source_target_pairs={{0,2},{2,0},{4,6},{6,4},{8,10},{10,8},{12,14},{14,12},{16,18},{18,... | collective-permute-start | bytes 884744 | tf_op jit(solution)/shard_map/ppermute | solution.py:519
  29.6 3.4 %collective-permute-start.9 = (bf16[4,96,384]{2,1,0:T(8,128)(2,1)S(1)}, bf16[4,96,384]{2,1,0:T(8,128)(2,1)S(1)}, u32[]{:S(2)}, u32[]{:S(2)}) collective-permute-start(bf16[4,96,384]{2,1,0:T(8,128)(2,1)S(1)} %collective-permute-done.3.n3), channel_id=1, source_target_pairs={{0,2},{2,0},{4,6},{6,4},{8,10},{10,8},{12,14},{14,12},{16,18},{18,... | collective-permute-start | bytes 884744 | tf_op jit(solution)/shard_map/ppermute | solution.py:519
  34.2 4.6 %attend_other.1 = (bf16[512,384]{1,0:T(8,128)(2,1)S(1)}, bf16[512,384]{1,0:T(8,128)(2,1)S(1)}, bf16[512,384]{1,0:T(8,128)(2,1)S(1)}, bf16[12,256,128]{2,1,0:T(8,...) custom-call(s32[5]{0:T(128)S(1)} %stack.23.me, ...), custom_call_target="tpu_custom_call" | custom-call | flops 1 | bytes 999999986991104 | tf_op jit(solution)/shard_map/attend_other/pallas_call | solution.py:55
  39.3 3.6 %feed_own.1 = (bf16[512,1536]{1,0:T(8,128)(2,1)S(1)}, bf16[512,1536]{1,0:T(8,128)(2,1)S(1)}, f32[512,768]{1,0:T(8,128)S(1)}, bf16[768,512]{1,0:T(8,128)(2,1)S(1)}) custom-call(s32[5]{0:T(128)S(1)} %stack.23.me, bf16[512,768]{1,0:T(8,128)(2,1)S(1)} %get-tuple-element.287.mid_low, bf16[768,1536]{1,0:T(8,128)(2,1)S(1)} %copy-done.1, ...), custom_call_target="tpu_custom_call" | custom-call | flops 1 | bytes 999999986991104 | tf_op jit(solution)/shard_map/feed_own/pallas_call | solution.py:55
  46.7 6.0 %feed_other.1 = (bf16[512,1536]{1,0:T(8,128)(2,1)S(1)}, bf16[512,1536]{1,0:T(8,128)(2,1)S(1)}, bf16[768,1536]{1,0:T(8,128)(2,1)S(1)}, bf16[1536,768]{1,0:T(8,128...) custom-call(s32[5]{0:T(128)S(1)} %stack.23.me, ...), custom_call_target="tpu_custom_call" | custom-call | flops 30000001024 | bytes 999999986991104 | tf_op jit(solution)/shard_map/feed_other/pallas_call | solution.py:55
  52.7 4.0 %back_grad.1 = (bf16[2,2,2,2,96,768]{5,4,3,2,1,0:T(8,128)(2,1)S(1)}, bf16[2,2,2,2,96,768]{5,4,3,2,1,0:T(8,128)(2,1)S(1)}) custom-call(s32[5]{0:T(128)S(1)} %stack.23.me, bf16[512,1536]{1,0:T(8,128)(2,1)S(1)} %get-tuple-element.311.hid_own, bf16[512,1536]{1,0:T(8,128)(2,1)S(1)} %get-tuple-element.312.hid_other, bf16[512,768]{1,0:T(8,128)(2,1)S(1)} %get-tuple-element.329.fed), custom_call_target="tpu_custom_call" | custom-call | flops 30000001024 | bytes 999999986991104 | tf_op jit(solution)/shard_map/back_grad/pallas_call | solution.py:55
  56.9 4.5 %in_grad_own.1 = (bf16[768,1536]{1,0:T(8,128)(2,1)S(1)}, f32[4,1,384]{2,1,0:T(1,128)S(1)}, f32[512,768]{1,0:T(8,128)S(1)}) custom-call(s32[5]{0:T(128)S(1)} %stack.23.me, bf16[768,512]{1,0:T(8,128)(2,1)S(1)} %get-tuple-element.328.mid_t, bf16[512,768]{1,0:T(8,128)(2,1)S(1)} %get-tuple-element.329.fed, bf16[1536,768]{1,0:T(8,128)(2,1)S(1)} %copy-done.2, ...), custom_call_target="tpu_custom_call" | custom-call | flops 30000001024 | bytes 999999986991104 | tf_op jit(solution)/shard_map/in_grad_own/pallas_call | solution.py:55
  64.3 5.7 %in_grad_other.1 = (bf16[2,2,2,2,192,384]{5,4,3,2,1,0:T(8,128)(2,1)S(1)}, bf16[2,2,2,2,192,384]{5,4,3,2,1,0:T(8,128)(2,1)S(1)}, f32[4,1,384]{2,1,0:T(1,128)S(1)}...) custom-call(s32[5]{0:T(128)S(1)} %stack.23.me, ...), custom_call_target="tpu_custom_call" | custom-call | flops 30000001024 | bytes 999999986991104 | tf_op jit(solution)/shard_map/in_grad_other/pallas_call | solution.py:55
  70.4 5.2 %attend_back.2 = (bf16[512,1152]{1,0:T(8,128)(2,1)S(1)}, bf16[2,384,384]{2,1,0:T(8,128)(2,1)S(1)}) custom-call(s32[5]{0:T(128)S(1)} %stack.23.me, bf16[512,768]{1,0:T(8,128)(2,1)S(1)} %get-tuple-element.361.grad_att, bf16[384,768]{1,0:T(8,128)(2,1)S(1)} %get-tuple-element.352.w_out, bf16[512,384]{1,0:T(8,128)(2,1)S(1)} %get-tuple-element.353.ctx, ...), custom_call_target="tpu_custom_call" | custom-call | flops 30000001024 | bytes 999999986991104 | tf_op jit(solution)/shard_map/attend_back/pallas_call | solution.py:55
  78.6 5.2 %attend_back.3 = (bf16[512,1152]{1,0:T(8,128)(2,1)S(1)}, bf16[2,384,384]{2,1,0:T(8,128)(2,1)S(1)}) custom-call(s32[5]{0:T(128)S(1)} %stack.23.me, bf16[512,768]{1,0:T(8,128)(2,1)S(1)} %get-tuple-element.361.grad_att, bf16[384,768]{1,0:T(8,128)(2,1)S(1)} %copy-done.5, bf16[512,384]{1,0:T(8,128)(2,1)S(1)} %copy-done.7, ...), custom_call_target="tpu_custom_call" | custom-call | flops 30000001024 | bytes 999999986991104 | tf_op jit(solution)/shard_map/attend_back/pallas_call | solution.py:55
  83.8 3.3 %qkv_grad.1 = (bf16[2,2,2,2,208,384]{5,4,3,2,1,0:T(8,128)(2,1)S(1)}, bf16[2,2,2,2,208,384]{5,4,3,2,1,0:T(8,128)(2,1)S(1)}) custom-call(s32[5]{0:T(128)S(1)} %stack.23.me, bf16[768,512]{1,0:T(8,128)(2,1)S(1)} %get-tuple-element.377.x_t, bf16[512,1152]{1,0:T(8,128)(2,1)S(1)} %get-tuple-element.398.own, bf16[2,384,384]{2,1,0:T(8,128)(2,1)S(1)} %get-tuple-element.379.own_out, ...), custom_call_target="tpu_custom_call" | custom-call | flops 30000001024 | bytes 999999986991104 | tf_op jit(solution)/shard_map/qkv_grad/pallas_call | solution.py:55
  94.9 6.8 %collective-permute-done.20.refs_3_ = bf16[2,2,96,768]{3,2,1,0:T(8,128)(2,1)S(1)} collective-permute-done((bf16[2,2,96,768]{3,2,1,0:T(8,128)(2,1)S(1)}, bf16[2,2,96,768]{3,2,1,0:T(8,128)(2,1)S(1)}, u32[]{:S(2)}, u32[]{:S(2)}) %collective-permute-start.20) | collective-permute-done | bytes 589856 | tf_op jit(solution)/shard_map/ppermute | solution.py:530
  102.5 4.1 %token_grad.1 = bf16[512,768]{1,0:T(8,128)(2,1)} custom-call(s32[5]{0:T(128)S(1)} %stack.23.me, f32[512,768]{1,0:T(8,128)S(1)} %get-tuple-element.397.grad_one, bf16[512,1152]{1,0:T(8,128)(2,1)S(1)} %get-tuple-element.398.own, bf16[512,1152]{1,0:T(8,128)(2,1)S(1)} %get-tuple-element.399.oth, bf16[3,768,384]{2,1,0:T(8,128)(2,1)S(1)} %copy-done.3, ...), custom_call_target="tpu_custom_call" | custom-call | flops 30000001024 | bytes 999999986991104 | tf_op jit(solution)/shard_map/token_grad/pallas_call | solution.py:55
  109.5 3.5 %collective-permute-done.23.refs_2_ = bf16[2,2,2,208,384]{4,3,2,1,0:T(8,128)(2,1)S(1)} collective-permute-done((bf16[2,2,2,208,384]{4,3,2,1,0:T(8,128)(2,1)S(1)}, bf16[2,2,2,208,384]{4,3,2,1,0:T(8,128)(2,1)S(1)}, u32[]{:S(2)}, u32[]{:S(2)}) %collective-permute-start.23) | collective-permute-done | bytes 1277984 | tf_op jit(solution)/shard_map/ppermute | solution.py:530
  115.5 3.9 %collective-permute-done.26.refs_3_ = bf16[2,2,192,384]{3,2,1,0:T(8,128)(2,1)S(1)} collective-permute-done((bf16[2,2,192,384]{3,2,1,0:T(8,128)(2,1)S(1)}, bf16[2,2,192,384]{3,2,1,0:T(8,128)(2,1)S(1)}, u32[]{:S(2)}, u32[]{:S(2)}) %collective-permute-start.26) | collective-permute-done | bytes 589856 | tf_op jit(solution)/shard_map/ppermute | solution.py:530
  120.1 6.1 %collective-permute-done.25.refs_3_ = bf16[2,2,208,384]{3,2,1,0:T(8,128)(2,1)S(1)} collective-permute-done((bf16[2,2,208,384]{3,2,1,0:T(8,128)(2,1)S(1)}, bf16[2,2,208,384]{3,2,1,0:T(8,128)(2,1)S(1)}, u32[]{:S(2)}, u32[]{:S(2)}) %collective-permute-start.25) | collective-permute-done | bytes 639008 | tf_op jit(solution)/shard_map/ppermute | solution.py:530
  130.1 3.4 %collective-permute-done.27.refs_4_ = bf16[2,208,384]{2,1,0:T(8,128)(2,1)S(1)} collective-permute-done((bf16[2,208,384]{2,1,0:T(8,128)(2,1)S(1)}, bf16[2,208,384]{2,1,0:T(8,128)(2,1)S(1)}, u32[]{:S(2)}, u32[]{:S(2)}) %collective-permute-start.27) | collective-permute-done | bytes 319520 | tf_op jit(solution)/shard_map/ppermute | solution.py:530
  134.4 3.4 %collective-permute-done.32.refs_1_ = bf16[2,192,384]{2,1,0:T(8,128)(2,1)S(1)} collective-permute-done((bf16[2,192,384]{2,1,0:T(8,128)(2,1)S(1)}, bf16[2,192,384]{2,1,0:T(8,128)(2,1)S(1)}, u32[]{:S(2)}, u32[]{:S(2)}) %collective-permute-start.32) | collective-permute-done | bytes 294944 | tf_op jit(solution)/shard_map/ppermute | solution.py:530
  140.1 5.9 %collective-permute-start.41 = (bf16[2,2,96,768]{3,2,1,0:T(8,128)(2,1)S(1)}, bf16[2,2,96,768]{3,2,1,0:T(8,128)(2,1)S(1)}, u32[]{:S(2)}, u32[]{:S(2)}) collective-permute-start(bf16[2,2,96,768]{3,2,1,0:T(8,128)(2,1)S(1)} %join.3.b0), channel_id=1, source_target_pairs={{0,4},{1,5},{2,10},{3,11},{4,0},{5,1},{6,14},{7,15},{8,12},{9,13},... | collective-permute-start | bytes 1769480 | tf_op jit(solution)/shard_map/ppermute | solution.py:530
  146.0 12.9 %collective-permute-start.35 = (bf16[2,2,96,768]{3,2,1,0:T(8,128)(2,1)S(1)}, bf16[2,2,96,768]{3,2,1,0:T(8,128)(2,1)S(1)}, u32[]{:S(2)}, u32[]{:S(2)}) collective-permute-start(bf16[2,2,96,768]{3,2,1,0:T(8,128)(2,1)S(1)} %join.3.b0), channel_id=1, source_target_pairs={{0,2},{2,0},{4,6},{6,4},{8,10},{10,8},{12,14},{14,12},{16,18},{18,... | collective-permute-start | bytes 1769480 | tf_op jit(solution)/shard_map/ppermute | solution.py:519
  162.0 4.6 %collective-permute-start.38 = (bf16[2,2,192,384]{3,2,1,0:T(8,128)(2,1)S(1)}, bf16[2,2,192,384]{3,2,1,0:T(8,128)(2,1)S(1)}, u32[]{:S(2)}, u32[]{:S(2)}) collective-permute-start(bf16[2,2,192,384]{3,2,1,0:T(8,128)(2,1)S(1)} %join.4.b0), channel_id=1, source_target_pairs={{0,2},{2,0},{4,6},{6,4},{8,10},{10,8},{12,14},{14,12},{16,18},{18,... | collective-permute-start | bytes 1769480 | tf_op jit(solution)/shard_map/ppermute | solution.py:519
  166.5 5.6 %collective-permute-start.42 = (bf16[2,2,96,768]{3,2,1,0:T(8,128)(2,1)S(1)}, bf16[2,2,96,768]{3,2,1,0:T(8,128)(2,1)S(1)}, u32[]{:S(2)}, u32[]{:S(2)}) collective-permute-start(bf16[2,2,96,768]{3,2,1,0:T(8,128)(2,1)S(1)} %collective-permute-done.41.b2), channel_id=1, source_target_pairs={{0,2},{2,0},{4,6},{6,4},{8,10},{10,8},{12,14},{14,12},{16,18},{18,... | collective-permute-start | bytes 1769480 | tf_op jit(solution)/shard_map/ppermute | solution.py:519
  173.8 4.6 %collective-permute-start.40 = (bf16[2,2,192,384]{3,2,1,0:T(8,128)(2,1)S(1)}, bf16[2,2,192,384]{3,2,1,0:T(8,128)(2,1)S(1)}, u32[]{:S(2)}, u32[]{:S(2)}) collective-permute-start(bf16[2,2,192,384]{3,2,1,0:T(8,128)(2,1)S(1)} %collective-permute-done.39.b2), channel_id=1, source_target_pairs={{0,2},{2,0},{4,6},{6,4},{8,10},{10,8},{12,14},{14,12},{16,18},{18,... | collective-permute-start | bytes 1769480 | tf_op jit(solution)/shard_map/ppermute | solution.py:519
  178.4 3.2 %place_back.1 = f32[1536,768]{1,0:T(8,128)} custom-call(s32[5]{0:T(128)S(1)} %stack.23.me, bf16[2,2,96,768]{3,2,1,0:T(8,128)(2,1)S(1)} %join.3.b0, bf16[2,2,96,768]{3,2,1,0:T(8,128)(2,1)S(1)} %collective-permute-done.35.b1, bf16[2,2,96,768]{3,2,1,0:T(8,128)(2,1)S(1)} %collective-permute-done.41.b2, bf16[2,2,96,768]{3,2,1,0:T(8,128)(2,1)S(1)} %collective-permute-done.42.b3), custom_call_target="tpu_custom_call" | custom-call | flops 30000001024 | bytes 999999986991104 | tf_op jit(solution)/shard_map/place_back/pallas_call | solution.py:55
  (149 shorter events, 71.5 us)
Async XLA Ops:
  4.9 18.0 %collective-permute-start.8 = (f32[6,1,384]{2,1,0:T(1,128)S(1)}, f32[6,1,384]{2,1,0:T(1,128)S(1)}, u32[]{:S(2)}, u32[]{:S(2)}) collective-permute-start(f32[6,1,384]{2,1,0:T(1,128)S(1)} %pack_biases.1.bias), channel_id=1, source_target_pairs={{0,1},{1,0},{2,3},{3,2},{4,5},{5,4},{6,7},{7,6},{8,9},{9,8},{10,11... | collective-permute-start | bytes 27656 | tf_op jit(solution)/shard_map/ppermute | solution.py:522
  7.6 16.6 %collective-permute-start.7 = (bf16[768,384]{1,0:T(8,128)(2,1)}, bf16[768,384]{1,0:T(8,128)(2,1)S(1)}, u32[]{:S(2)}, u32[]{:S(2)}) collective-permute-start(bf16[768,384]{1,0:T(8,128)(2,1)} %pack_feed.1), channel_id=1, source_target_pairs={{0,1},{1,0},{2,3},{3,2},{4,5},{5,4},{6,7},{7,6},{8,9},{9,8},{10,11... | collective-permute-start | bytes 1769480 | tf_op jit(solution)/shard_map/ppermute | solution.py:522
  11.1 9.0 %collective-permute-start.2 = (bf16[4,96,384]{2,1,0:T(8,128)(2,1)S(1)}, bf16[4,96,384]{2,1,0:T(8,128)(2,1)S(1)}, u32[]{:S(2)}, u32[]{:S(2)}) collective-permute-start(bf16[4,96,384]{2,1,0:T(8,128)(2,1)S(1)} %collective-permute-done.n0), channel_id=1, source_target_pairs={{0,4},{2,6},{4,0},{6,2},{8,12},{10,14},{12,8},{14,10},{16,20},{18,... | collective-permute-start | bytes 884744 | tf_op jit(solution)/shard_map/ppermute | solution.py:519
  24.2 18.7 %collective-permute-start.11 = (bf16[768,384]{1,0:T(8,128)(2,1)S(1)}, bf16[768,384]{1,0:T(8,128)(2,1)S(1)}, u32[]{:S(2)}, u32[]{:S(2)}) collective-permute-start(bf16[768,384]{1,0:T(8,128)(2,1)S(1)} %collective-permute-done.7.f0), channel_id=1, source_target_pairs={{0,4},{2,6},{4,0},{6,2},{8,12},{10,14},{12,8},{14,10},{16,20},{18,... | collective-permute-start | bytes 1769480 | tf_op jit(solution)/shard_map/ppermute | solution.py:519
  25.2 17.7 %collective-permute-start.10 = (bf16[768,384]{1,0:T(8,128)(2,1)S(1)}, bf16[768,384]{1,0:T(8,128)(2,1)S(1)}, u32[]{:S(2)}, u32[]{:S(2)}) collective-permute-start(bf16[768,384]{1,0:T(8,128)(2,1)S(1)} %collective-permute-done.7.f0), channel_id=1, source_target_pairs={{0,8},{2,10},{4,12},{6,14},{8,0},{10,2},{12,4},{14,6},{16,24},{18,... | collective-permute-start | bytes 1769480 | tf_op jit(solution)/shard_map/ppermute | solution.py:519
  28.3 15.2 %collective-permute-start.12 = (bf16[768,384]{1,0:T(8,128)(2,1)S(1)}, bf16[768,384]{1,0:T(8,128)(2,1)S(1)}, u32[]{:S(2)}, u32[]{:S(2)}) collective-permute-start(bf16[768,384]{1,0:T(8,128)(2,1)S(1)} %pack_feed_d.1), channel_id=1, source_target_pairs={{0,1},{1,0},{2,3},{3,2},{4,5},{5,4},{6,7},{7,6},{8,9},{9,8},{10,11... | collective-permute-start | bytes 1769480 | tf_op jit(solution)/shard_map/ppermute | solution.py:522
  62.7 15.8 %collective-permute-start.19 = (bf16[2,2,2,96,768]{4,3,2,1,0:T(8,128)(2,1)S(1)}, bf16[2,2,2,96,768]{4,3,2,1,0:T(8,128)(2,1)S(1)}, u32[]{:S(2)}, u32[]{:S(2)}) collective-permute-start(bf16[2,2,2,96,768]{4,3,2,1,0:T(8,128)(2,1)S(1)} %add_half.9), channel_id=1, source_target_pairs={{0,1},{1,0},{2,10},{3,11},{4,5},{5,4},{6,14},{7,15},{8,9},{9,8},{1... | collective-permute-start | bytes 3538952 | tf_op jit(solution)/shard_map/ppermute | solution.py:530
  77.0 24.7 %collective-permute-start.22 = (bf16[2,2,2,192,384]{4,3,2,1,0:T(8,128)(2,1)S(1)}, bf16[2,2,2,192,384]{4,3,2,1,0:T(8,128)(2,1)S(1)}, u32[]{:S(2)}, u32[]{:S(2)}) collective-permute-start(bf16[2,2,2,192,384]{4,3,2,1,0:T(8,128)(2,1)S(1)} %add_half.10), channel_id=1, source_target_pairs={{0,1},{1,0},{2,10},{3,11},{4,5},{5,4},{6,14},{7,15},{8,9},{9,8},{1... | collective-permute-start | bytes 3538952 | tf_op jit(solution)/shard_map/ppermute | solution.py:530
  88.7 13.0 %collective-permute-start.20 = (bf16[2,2,96,768]{3,2,1,0:T(8,128)(2,1)S(1)}, bf16[2,2,96,768]{3,2,1,0:T(8,128)(2,1)S(1)}, u32[]{:S(2)}, u32[]{:S(2)}) collective-permute-start(bf16[2,2,96,768]{3,2,1,0:T(8,128)(2,1)S(1)} %add_half.11), channel_id=1, source_target_pairs={{0,4},{1,5},{2,3},{3,2},{4,0},{5,1},{6,7},{7,6},{8,12},{9,13},{10,... | collective-permute-start | bytes 1769480 | tf_op jit(solution)/shard_map/ppermute | solution.py:530
  93.3 19.8 %collective-permute-start.23 = (bf16[2,2,2,208,384]{4,3,2,1,0:T(8,128)(2,1)S(1)}, bf16[2,2,2,208,384]{4,3,2,1,0:T(8,128)(2,1)S(1)}, u32[]{:S(2)}, u32[]{:S(2)}) collective-permute-start(bf16[2,2,2,208,384]{4,3,2,1,0:T(8,128)(2,1)S(1)} %add_half.12), channel_id=1, source_target_pairs={{0,1},{1,0},{2,10},{3,11},{4,5},{5,4},{6,14},{7,15},{8,9},{9,8},{1... | collective-permute-start | bytes 3833864 | tf_op jit(solution)/shard_map/ppermute | solution.py:530
  107.3 12.0 %collective-permute-start.26 = (bf16[2,2,192,384]{3,2,1,0:T(8,128)(2,1)S(1)}, bf16[2,2,192,384]{3,2,1,0:T(8,128)(2,1)S(1)}, u32[]{:S(2)}, u32[]{:S(2)}) collective-permute-start(bf16[2,2,192,384]{3,2,1,0:T(8,128)(2,1)S(1)} %add_half.14), channel_id=1, source_target_pairs={{0,4},{1,5},{2,3},{3,2},{4,0},{5,1},{6,7},{7,6},{8,12},{9,13},{10,... | collective-permute-start | bytes 1769480 | tf_op jit(solution)/shard_map/ppermute | solution.py:530
  109.4 17.6 %collective-permute-start.29 = (bf16[2,96,768]{2,1,0:T(8,128)(2,1)S(1)}, bf16[2,96,768]{2,1,0:T(8,128)(2,1)S(1)}, u32[]{:S(2)}, u32[]{:S(2)}) collective-permute-start(bf16[2,96,768]{2,1,0:T(8,128)(2,1)S(1)} %add_all.3.refs_0_), channel_id=1, source_target_pairs={{0,16},{1,17},{2,18},{3,19},{4,20},{5,21},{6,22},{7,23},{8,24},{9,... | collective-permute-start | bytes 884744 | tf_op jit(solution)/shard_map/ppermute | solution.py:530
  113.9 12.3 %collective-permute-start.25 = (bf16[2,2,208,384]{3,2,1,0:T(8,128)(2,1)S(1)}, bf16[2,2,208,384]{3,2,1,0:T(8,128)(2,1)S(1)}, u32[]{:S(2)}, u32[]{:S(2)}) collective-permute-start(bf16[2,2,208,384]{3,2,1,0:T(8,128)(2,1)S(1)} %add_half.15), channel_id=1, source_target_pairs={{0,4},{1,5},{2,3},{3,2},{4,0},{5,1},{6,7},{7,6},{8,12},{9,13},{10,... | collective-permute-start | bytes 1916936 | tf_op jit(solution)/shard_map/ppermute | solution.py:530
  120.0 9.2 %collective-permute-start.28 = (bf16[2,192,384]{2,1,0:T(8,128)(2,1)S(1)}, bf16[2,192,384]{2,1,0:T(8,128)(2,1)S(1)}, u32[]{:S(2)}, u32[]{:S(2)}) collective-permute-start(bf16[2,192,384]{2,1,0:T(8,128)(2,1)S(1)} %add_half.16), channel_id=1, source_target_pairs={{0,8},{1,9},{2,6},{3,7},{4,12},{5,13},{6,2},{7,3},{8,0},{9,1},{10,... | collective-permute-start | bytes 884744 | tf_op jit(solution)/shard_map/ppermute | solution.py:530
  127.6 10.2 %collective-permute-start.31 = (bf16[2,96,768]{2,1,0:T(8,128)(2,1)S(1)}, bf16[2,96,768]{2,1,0:T(8,128)(2,1)S(1)}, u32[]{:S(2)}, u32[]{:S(2)}) collective-permute-start(bf16[2,96,768]{2,1,0:T(8,128)(2,1)S(1)} %add_two.3.a), channel_id=1, source_target_pairs={{0,8},{1,9},{2,6},{3,7},{4,12},{5,13},{6,2},{7,3},{8,0},{9,1},{10,... | collective-permute-start | bytes 884744 | tf_op jit(solution)/shard_map/ppermute | solution.py:530
  134.2 24.7 %collective-permute-start.30 = (bf16[2,208,384]{2,1,0:T(8,128)(2,1)S(1)}, bf16[2,208,384]{2,1,0:T(8,128)(2,1)S(1)}, u32[]{:S(2)}, u32[]{:S(2)}) collective-permute-start(bf16[2,208,384]{2,1,0:T(8,128)(2,1)S(1)} %add_all.5.refs_0_), channel_id=1, source_target_pairs={{0,16},{1,17},{2,18},{3,19},{4,20},{5,21},{6,22},{7,23},{8,24},{9,... | collective-permute-start | bytes 958472 | tf_op jit(solution)/shard_map/ppermute | solution.py:530
  138.4 22.9 %collective-permute-start.34 = (bf16[2,192,384]{2,1,0:T(8,128)(2,1)S(1)}, bf16[2,192,384]{2,1,0:T(8,128)(2,1)S(1)}, u32[]{:S(2)}, u32[]{:S(2)}) collective-permute-start(bf16[2,192,384]{2,1,0:T(8,128)(2,1)S(1)} %add_two.4.a), channel_id=1, source_target_pairs={{0,8},{1,9},{2,6},{3,7},{4,12},{5,13},{6,2},{7,3},{8,0},{9,1},{10,... | collective-permute-start | bytes 884744 | tf_op jit(solution)/shard_map/ppermute | solution.py:530
  140.1 26.4 %collective-permute-start.41 = (bf16[2,2,96,768]{3,2,1,0:T(8,128)(2,1)S(1)}, bf16[2,2,96,768]{3,2,1,0:T(8,128)(2,1)S(1)}, u32[]{:S(2)}, u32[]{:S(2)}) collective-permute-start(bf16[2,2,96,768]{3,2,1,0:T(8,128)(2,1)S(1)} %join.3.b0), channel_id=1, source_target_pairs={{0,4},{1,5},{2,10},{3,11},{4,0},{5,1},{6,14},{7,15},{8,12},{9,13},... | collective-permute-start | bytes 1769480 | tf_op jit(solution)/shard_map/ppermute | solution.py:530
  146.0 15.3 %collective-permute-start.35 = (bf16[2,2,96,768]{3,2,1,0:T(8,128)(2,1)S(1)}, bf16[2,2,96,768]{3,2,1,0:T(8,128)(2,1)S(1)}, u32[]{:S(2)}, u32[]{:S(2)}) collective-permute-start(bf16[2,2,96,768]{3,2,1,0:T(8,128)(2,1)S(1)} %join.3.b0), channel_id=1, source_target_pairs={{0,2},{2,0},{4,6},{6,4},{8,10},{10,8},{12,14},{14,12},{16,18},{18,... | collective-permute-start | bytes 1769480 | tf_op jit(solution)/shard_map/ppermute | solution.py:519
  159.5 12.6 %collective-permute-start.33 = (bf16[2,208,384]{2,1,0:T(8,128)(2,1)S(1)}, bf16[2,208,384]{2,1,0:T(8,128)(2,1)S(1)}, u32[]{:S(2)}, u32[]{:S(2)}) collective-permute-start(bf16[2,208,384]{2,1,0:T(8,128)(2,1)S(1)} %add_two.5.a), channel_id=1, source_target_pairs={{0,8},{1,9},{2,6},{3,7},{4,12},{5,13},{6,2},{7,3},{8,0},{9,1},{10,... | collective-permute-start | bytes 958472 | tf_op jit(solution)/shard_map/ppermute | solution.py:530
  161.9 12.0 %collective-permute-start.39 = (bf16[2,2,192,384]{3,2,1,0:T(8,128)(2,1)S(1)}, bf16[2,2,192,384]{3,2,1,0:T(8,128)(2,1)S(1)}, u32[]{:S(2)}, u32[]{:S(2)}) collective-permute-start(bf16[2,2,192,384]{3,2,1,0:T(8,128)(2,1)S(1)} %join.4.b0), channel_id=1, source_target_pairs={{0,4},{1,5},{2,10},{3,11},{4,0},{5,1},{6,14},{7,15},{8,12},{9,13},... | collective-permute-start | bytes 1769480 | tf_op jit(solution)/shard_map/ppermute | solution.py:530
  162.0 11.8 %collective-permute-start.38 = (bf16[2,2,192,384]{3,2,1,0:T(8,128)(2,1)S(1)}, bf16[2,2,192,384]{3,2,1,0:T(8,128)(2,1)S(1)}, u32[]{:S(2)}, u32[]{:S(2)}) collective-permute-start(bf16[2,2,192,384]{3,2,1,0:T(8,128)(2,1)S(1)} %join.4.b0), channel_id=1, source_target_pairs={{0,2},{2,0},{4,6},{6,4},{8,10},{10,8},{12,14},{14,12},{16,18},{18,... | collective-permute-start | bytes 1769480 | tf_op jit(solution)/shard_map/ppermute | solution.py:519
  172.7 12.1 %collective-permute-start.37 = (bf16[2,2,208,384]{3,2,1,0:T(8,128)(2,1)S(1)}, bf16[2,2,208,384]{3,2,1,0:T(8,128)(2,1)S(1)}, u32[]{:S(2)}, u32[]{:S(2)}) collective-permute-start(bf16[2,2,208,384]{3,2,1,0:T(8,128)(2,1)S(1)} %join.5.b0), channel_id=1, source_target_pairs={{0,4},{1,5},{2,10},{3,11},{4,0},{5,1},{6,14},{7,15},{8,12},{9,13},... | collective-permute-start | bytes 1916936 | tf_op jit(solution)/shard_map/ppermute | solution.py:530
  172.8 8.8 %collective-permute-start.36 = (bf16[2,2,208,384]{3,2,1,0:T(8,128)(2,1)S(1)}, bf16[2,2,208,384]{3,2,1,0:T(8,128)(2,1)S(1)}, u32[]{:S(2)}, u32[]{:S(2)}) collective-permute-start(bf16[2,2,208,384]{3,2,1,0:T(8,128)(2,1)S(1)} %join.5.b0), channel_id=1, source_target_pairs={{0,2},{2,0},{4,6},{6,4},{8,10},{10,8},{12,14},{14,12},{16,18},{18,... | collective-permute-start | bytes 1916936 | tf_op jit(solution)/shard_map/ppermute | solution.py:519
  (41 other events, 263.1 us)

commit v2 on v1

--- a/solution.py
+++ b/solution.py
@@ -64,7 +64,7 @@
     )(me, *ins)
 
 
-def packed(body, name, me, ins, outs):
+def packed(body, name, me, ins, outs, cost=COST):
     return pl.pallas_call(
         body,
         name=name,
@@ -73,7 +73,7 @@
         out_specs=[vmem()] * len(outs),
         scratch_shapes=[pltpu.SemaphoreType.DMA((3,))],
         compiler_params=pltpu.CompilerParams(vmem_limit_bytes=LIMIT * MB),
-        cost_estimate=COST,
+        cost_estimate=cost,
     )(me, *[pltpu.with_memory_space_constraint(v, pltpu.HBM) for v in ins])
 
 
@@ -554,7 +554,7 @@
 
     near_shape = sds((4, model // 8, half))
     feed_shape = sds((model, quarter))
-    near, = packed(functools.partial(pack_attn, False), "pack_near", me, (w_qkv, w_out), [near_shape])
+    near, = packed(functools.partial(pack_attn, False), "pack_near", me, (w_qkv, w_out), [near_shape], LITTLE)
     near_y = over_tensor(near)
     clock[0] = near
     biases, = kernel(pack_biases, "pack_biases", (attn_bias, ffn_bias), [sds((6, 1, quarter), f32)])

time: 193 us -> 193 us (level)
  transfers between devices with their start and end apart: 44 -> 44, of which waited for: 16 -> 15; matrix products, arithmetic and copies ran while one was open for 0% -> 0% of each run, Pallas kernels for 33% -> 33%
where the time goes in v2:
time: 193 us; the launch traced here: 189 us
  Pallas kernels  78.9 us (41%)
  starting transfers between devices  70.2 us (36%)
  waiting for transfers between devices  36.5 us (19%)
  between operations  2.03 us (1%)
    pallas_call x34, Pallas kernels, call(): pl.pallas_call(body, name=name, out_shape=outs, in_specs=[smem()] + [vmem...  73.1 us
    ppermute x21, starting transfers between devices, over_dp(): return lax.ppermute(value, 'dp', [(i, i ^ 1 << b) for i in range(dp_size)])  45.4 us
    ppermute x19, waiting for transfers between devices, flip(): return lax.ppermute(value, ('dp', 'tensor'), pairs)  27.4 us
    ppermute x19, starting transfers between devices, flip(): return lax.ppermute(value, ('dp', 'tensor'), pairs)  20.6 us
    ppermute x21, waiting for transfers between devices, over_dp(): return lax.ppermute(value, 'dp', [(i, i ^ 1 << b) for i in range(dp_size)])  8.29 us
    pallas_call x3, Pallas kernels, packed(): pl.pallas_call(body, name=name, out_shape=outs, in_specs=[smem()] + [pl.B...  5.78 us
    ppermute x4, starting transfers between devices, over_tensor(): return lax.ppermute(value, 'tensor', [(0, 1), (1, 0)])  4.21 us
  transfers between devices with their start and end apart: 44, of which 15 were waited for; matrix products, arithmetic and copies ran while one was open for 0% of the time, Pallas kernels for 33%

profile of v2, /device:TPU:17, one launch (start us, length us, event | category | flops | bytes accessed | tf_op | source)
XLA Modules:
  0.0 189.4 jit_solution(17657441058315796740)
XLA Ops:
  15.9 3.3 %collective-permute-start.4 = (bf16[4,96,384]{2,1,0:T(8,128)(2,1)S(1)}, bf16[4,96,384]{2,1,0:T(8,128)(2,1)S(1)}, u32[]{:S(2)}, u32[]{:S(2)}) collective-permute-start(bf16[4,96,384]{2,1,0:T(8,128)(2,1)S(1)} %collective-permute-done.n0), channel_id=1, source_target_pairs={{0,2},{2,0},{4,6},{6,4},{8,10},{10,8},{12,14},{14,12},{16,18},{18,... | collective-permute-start | bytes 884744 | tf_op jit(solution)/shard_map/ppermute | solution.py:519
  33.2 4.6 %attend_other.1 = (bf16[512,384]{1,0:T(8,128)(2,1)S(1)}, bf16[512,384]{1,0:T(8,128)(2,1)S(1)}, bf16[512,384]{1,0:T(8,128)(2,1)S(1)}, bf16[12,256,128]{2,1,0:T(8,...) custom-call(s32[5]{0:T(128)S(1)} %stack.23.me, ...), custom_call_target="tpu_custom_call" | custom-call | flops 1 | bytes 999999986991104 | tf_op jit(solution)/shard_map/attend_other/pallas_call | solution.py:55
  38.2 3.6 %feed_own.1 = (bf16[512,1536]{1,0:T(8,128)(2,1)S(1)}, bf16[512,1536]{1,0:T(8,128)(2,1)S(1)}, f32[512,768]{1,0:T(8,128)S(1)}, bf16[768,512]{1,0:T(8,128)(2,1)S(1)}) custom-call(s32[5]{0:T(128)S(1)} %stack.23.me, bf16[512,768]{1,0:T(8,128)(2,1)S(1)} %get-tuple-element.287.mid_low, bf16[768,1536]{1,0:T(8,128)(2,1)S(1)} %copy-done.4, ...), custom_call_target="tpu_custom_call" | custom-call | flops 1 | bytes 999999986991104 | tf_op jit(solution)/shard_map/feed_own/pallas_call | solution.py:55
  45.6 6.5 %feed_other.1 = (bf16[512,1536]{1,0:T(8,128)(2,1)S(1)}, bf16[512,1536]{1,0:T(8,128)(2,1)S(1)}, bf16[768,1536]{1,0:T(8,128)(2,1)S(1)}, bf16[1536,768]{1,0:T(8,128...) custom-call(s32[5]{0:T(128)S(1)} %stack.23.me, ...), custom_call_target="tpu_custom_call" | custom-call | flops 30000001024 | bytes 999999986991104 | tf_op jit(solution)/shard_map/feed_other/pallas_call | solution.py:55
  52.2 4.0 %back_grad.1 = (bf16[2,2,2,2,96,768]{5,4,3,2,1,0:T(8,128)(2,1)S(1)}, bf16[2,2,2,2,96,768]{5,4,3,2,1,0:T(8,128)(2,1)S(1)}) custom-call(s32[5]{0:T(128)S(1)} %stack.23.me, bf16[512,1536]{1,0:T(8,128)(2,1)S(1)} %get-tuple-element.311.hid_own, bf16[512,1536]{1,0:T(8,128)(2,1)S(1)} %get-tuple-element.312.hid_other, bf16[512,768]{1,0:T(8,128)(2,1)S(1)} %get-tuple-element.329.fed), custom_call_target="tpu_custom_call" | custom-call | flops 30000001024 | bytes 999999986991104 | tf_op jit(solution)/shard_map/back_grad/pallas_call | solution.py:55
  56.3 4.4 %in_grad_own.1 = (bf16[768,1536]{1,0:T(8,128)(2,1)S(1)}, f32[4,1,384]{2,1,0:T(1,128)S(1)}, f32[512,768]{1,0:T(8,128)S(1)}) custom-call(s32[5]{0:T(128)S(1)} %stack.23.me, bf16[768,512]{1,0:T(8,128)(2,1)S(1)} %get-tuple-element.328.mid_t, bf16[512,768]{1,0:T(8,128)(2,1)S(1)} %get-tuple-element.329.fed, bf16[1536,768]{1,0:T(8,128)(2,1)S(1)} %copy-done.5, ...), custom_call_target="tpu_custom_call" | custom-call | flops 30000001024 | bytes 999999986991104 | tf_op jit(solution)/shard_map/in_grad_own/pallas_call | solution.py:55
  63.7 5.7 %in_grad_other.1 = (bf16[2,2,2,2,192,384]{5,4,3,2,1,0:T(8,128)(2,1)S(1)}, bf16[2,2,2,2,192,384]{5,4,3,2,1,0:T(8,128)(2,1)S(1)}, f32[4,1,384]{2,1,0:T(1,128)S(1)}...) custom-call(s32[5]{0:T(128)S(1)} %stack.23.me, ...), custom_call_target="tpu_custom_call" | custom-call | flops 30000001024 | bytes 999999986991104 | tf_op jit(solution)/shard_map/in_grad_other/pallas_call | solution.py:55
  69.8 5.2 %attend_back.2 = (bf16[512,1152]{1,0:T(8,128)(2,1)S(1)}, bf16[2,384,384]{2,1,0:T(8,128)(2,1)S(1)}) custom-call(s32[5]{0:T(128)S(1)} %stack.23.me, bf16[512,768]{1,0:T(8,128)(2,1)S(1)} %get-tuple-element.361.grad_att, bf16[384,768]{1,0:T(8,128)(2,1)S(1)} %get-tuple-element.352.w_out, bf16[512,384]{1,0:T(8,128)(2,1)S(1)} %get-tuple-element.353.ctx, ...), custom_call_target="tpu_custom_call" | custom-call | flops 30000001024 | bytes 999999986991104 | tf_op jit(solution)/shard_map/attend_back/pallas_call | solution.py:55
  77.9 5.2 %attend_back.3 = (bf16[512,1152]{1,0:T(8,128)(2,1)S(1)}, bf16[2,384,384]{2,1,0:T(8,128)(2,1)S(1)}) custom-call(s32[5]{0:T(128)S(1)} %stack.23.me, bf16[512,768]{1,0:T(8,128)(2,1)S(1)} %get-tuple-element.361.grad_att, bf16[384,768]{1,0:T(8,128)(2,1)S(1)} %copy-done.3, bf16[512,384]{1,0:T(8,128)(2,1)S(1)} %copy-done.7, ...), custom_call_target="tpu_custom_call" | custom-call | flops 30000001024 | bytes 999999986991104 | tf_op jit(solution)/shard_map/attend_back/pallas_call | solution.py:55
  83.2 3.3 %qkv_grad.1 = (bf16[2,2,2,2,208,384]{5,4,3,2,1,0:T(8,128)(2,1)S(1)}, bf16[2,2,2,2,208,384]{5,4,3,2,1,0:T(8,128)(2,1)S(1)}) custom-call(s32[5]{0:T(128)S(1)} %stack.23.me, bf16[768,512]{1,0:T(8,128)(2,1)S(1)} %get-tuple-element.377.x_t, bf16[512,1152]{1,0:T(8,128)(2,1)S(1)} %get-tuple-element.398.own, bf16[2,384,384]{2,1,0:T(8,128)(2,1)S(1)} %get-tuple-element.379.own_out, ...), custom_call_target="tpu_custom_call" | custom-call | flops 30000001024 | bytes 999999986991104 | tf_op jit(solution)/shard_map/qkv_grad/pallas_call | solution.py:55
  94.2 6.7 %collective-permute-done.20.refs_3_ = bf16[2,2,96,768]{3,2,1,0:T(8,128)(2,1)S(1)} collective-permute-done((bf16[2,2,96,768]{3,2,1,0:T(8,128)(2,1)S(1)}, bf16[2,2,96,768]{3,2,1,0:T(8,128)(2,1)S(1)}, u32[]{:S(2)}, u32[]{:S(2)}) %collective-permute-start.20) | collective-permute-done | bytes 589856 | tf_op jit(solution)/shard_map/ppermute | solution.py:530
  101.7 4.1 %token_grad.1 = bf16[512,768]{1,0:T(8,128)(2,1)} custom-call(s32[5]{0:T(128)S(1)} %stack.23.me, f32[512,768]{1,0:T(8,128)S(1)} %get-tuple-element.397.grad_one, bf16[512,1152]{1,0:T(8,128)(2,1)S(1)} %get-tuple-element.398.own, bf16[512,1152]{1,0:T(8,128)(2,1)S(1)} %get-tuple-element.399.oth, bf16[3,768,384]{2,1,0:T(8,128)(2,1)S(1)} %copy-done, ...), custom_call_target="tpu_custom_call" | custom-call | flops 30000001024 | bytes 999999986991104 | tf_op jit(solution)/shard_map/token_grad/pallas_call | solution.py:55
  108.8 3.6 %collective-permute-done.23.refs_2_ = bf16[2,2,2,208,384]{4,3,2,1,0:T(8,128)(2,1)S(1)} collective-permute-done((bf16[2,2,2,208,384]{4,3,2,1,0:T(8,128)(2,1)S(1)}, bf16[2,2,2,208,384]{4,3,2,1,0:T(8,128)(2,1)S(1)}, u32[]{:S(2)}, u32[]{:S(2)}) %collective-permute-start.23) | collective-permute-done | bytes 1277984 | tf_op jit(solution)/shard_map/ppermute | solution.py:530
  114.7 3.9 %collective-permute-done.26.refs_3_ = bf16[2,2,192,384]{3,2,1,0:T(8,128)(2,1)S(1)} collective-permute-done((bf16[2,2,192,384]{3,2,1,0:T(8,128)(2,1)S(1)}, bf16[2,2,192,384]{3,2,1,0:T(8,128)(2,1)S(1)}, u32[]{:S(2)}, u32[]{:S(2)}) %collective-permute-start.26) | collective-permute-done | bytes 589856 | tf_op jit(solution)/shard_map/ppermute | solution.py:530
  119.4 6.1 %collective-permute-done.25.refs_3_ = bf16[2,2,208,384]{3,2,1,0:T(8,128)(2,1)S(1)} collective-permute-done((bf16[2,2,208,384]{3,2,1,0:T(8,128)(2,1)S(1)}, bf16[2,2,208,384]{3,2,1,0:T(8,128)(2,1)S(1)}, u32[]{:S(2)}, u32[]{:S(2)}) %collective-permute-start.25) | collective-permute-done | bytes 639008 | tf_op jit(solution)/shard_map/ppermute | solution.py:530
  129.4 3.5 %collective-permute-done.27.refs_4_ = bf16[2,208,384]{2,1,0:T(8,128)(2,1)S(1)} collective-permute-done((bf16[2,208,384]{2,1,0:T(8,128)(2,1)S(1)}, bf16[2,208,384]{2,1,0:T(8,128)(2,1)S(1)}, u32[]{:S(2)}, u32[]{:S(2)}) %collective-permute-start.27) | collective-permute-done | bytes 319520 | tf_op jit(solution)/shard_map/ppermute | solution.py:530
  133.7 3.6 %collective-permute-done.32.refs_1_ = bf16[2,192,384]{2,1,0:T(8,128)(2,1)S(1)} collective-permute-done((bf16[2,192,384]{2,1,0:T(8,128)(2,1)S(1)}, bf16[2,192,384]{2,1,0:T(8,128)(2,1)S(1)}, u32[]{:S(2)}, u32[]{:S(2)}) %collective-permute-start.32) | collective-permute-done | bytes 294944 | tf_op jit(solution)/shard_map/ppermute | solution.py:530
  139.8 5.3 %collective-permute-start.41 = (bf16[2,2,96,768]{3,2,1,0:T(8,128)(2,1)S(1)}, bf16[2,2,96,768]{3,2,1,0:T(8,128)(2,1)S(1)}, u32[]{:S(2)}, u32[]{:S(2)}) collective-permute-start(bf16[2,2,96,768]{3,2,1,0:T(8,128)(2,1)S(1)} %join.3.b0), channel_id=1, source_target_pairs={{0,4},{1,5},{2,10},{3,11},{4,0},{5,1},{6,14},{7,15},{8,12},{9,13},... | collective-permute-start | bytes 1769480 | tf_op jit(solution)/shard_map/ppermute | solution.py:530
  145.1 13.2 %collective-permute-start.35 = (bf16[2,2,96,768]{3,2,1,0:T(8,128)(2,1)S(1)}, bf16[2,2,96,768]{3,2,1,0:T(8,128)(2,1)S(1)}, u32[]{:S(2)}, u32[]{:S(2)}) collective-permute-start(bf16[2,2,96,768]{3,2,1,0:T(8,128)(2,1)S(1)} %join.3.b0), channel_id=1, source_target_pairs={{0,2},{2,0},{4,6},{6,4},{8,10},{10,8},{12,14},{14,12},{16,18},{18,... | collective-permute-start | bytes 1769480 | tf_op jit(solution)/shard_map/ppermute | solution.py:519
  161.3 4.3 %collective-permute-start.38 = (bf16[2,2,192,384]{3,2,1,0:T(8,128)(2,1)S(1)}, bf16[2,2,192,384]{3,2,1,0:T(8,128)(2,1)S(1)}, u32[]{:S(2)}, u32[]{:S(2)}) collective-permute-start(bf16[2,2,192,384]{3,2,1,0:T(8,128)(2,1)S(1)} %join.4.b0), channel_id=1, source_target_pairs={{0,2},{2,0},{4,6},{6,4},{8,10},{10,8},{12,14},{14,12},{16,18},{18,... | collective-permute-start | bytes 1769480 | tf_op jit(solution)/shard_map/ppermute | solution.py:519
  165.6 5.9 %collective-permute-start.42 = (bf16[2,2,96,768]{3,2,1,0:T(8,128)(2,1)S(1)}, bf16[2,2,96,768]{3,2,1,0:T(8,128)(2,1)S(1)}, u32[]{:S(2)}, u32[]{:S(2)}) collective-permute-start(bf16[2,2,96,768]{3,2,1,0:T(8,128)(2,1)S(1)} %collective-permute-done.41.b2), channel_id=1, source_target_pairs={{0,2},{2,0},{4,6},{6,4},{8,10},{10,8},{12,14},{14,12},{16,18},{18,... | collective-permute-start | bytes 1769480 | tf_op jit(solution)/shard_map/ppermute | solution.py:519
  173.1 4.7 %collective-permute-start.40 = (bf16[2,2,192,384]{3,2,1,0:T(8,128)(2,1)S(1)}, bf16[2,2,192,384]{3,2,1,0:T(8,128)(2,1)S(1)}, u32[]{:S(2)}, u32[]{:S(2)}) collective-permute-start(bf16[2,2,192,384]{3,2,1,0:T(8,128)(2,1)S(1)} %collective-permute-done.39.b2), channel_id=1, source_target_pairs={{0,2},{2,0},{4,6},{6,4},{8,10},{10,8},{12,14},{14,12},{16,18},{18,... | collective-permute-start | bytes 1769480 | tf_op jit(solution)/shard_map/ppermute | solution.py:519
  177.8 3.2 %place_back.1 = f32[1536,768]{1,0:T(8,128)} custom-call(s32[5]{0:T(128)S(1)} %stack.23.me, bf16[2,2,96,768]{3,2,1,0:T(8,128)(2,1)S(1)} %join.3.b0, bf16[2,2,96,768]{3,2,1,0:T(8,128)(2,1)S(1)} %collective-permute-done.35.b1, bf16[2,2,96,768]{3,2,1,0:T(8,128)(2,1)S(1)} %collective-permute-done.41.b2, bf16[2,2,96,768]{3,2,1,0:T(8,128)(2,1)S(1)} %collective-permute-done.42.b3), custom_call_target="tpu_custom_call" | custom-call | flops 30000001024 | bytes 999999986991104 | tf_op jit(solution)/shard_map/place_back/pallas_call | solution.py:55
  181.0 3.2 %place_in.1 = f32[768,1536]{1,0:T(8,128)} custom-call(s32[5]{0:T(128)S(1)} %stack.23.me, bf16[2,2,192,384]{3,2,1,0:T(8,128)(2,1)S(1)} %join.4.b0, bf16[2,2,192,384]{3,2,1,0:T(8,128)(2,1)S(1)} %collective-permute-done.38.b1, bf16[2,2,192,384]{3,2,1,0:T(8,128)(2,1)S(1)} %collective-permute-done.39.b2, bf16[2,2,192,384]{3,2,1,0:T(8,128)(2,1)S(1)} %collective-permute-done.40.b3), custom_call_target="tpu_custom_call" | custom-call | flops 30000001024 | bytes 999999986991104 | tf_op jit(solution)/shard_map/place_in/pallas_call | solution.py:55
  (149 shorter events, 70.5 us)
Async XLA Ops:
  4.2 17.8 %collective-permute-start.8 = (f32[6,1,384]{2,1,0:T(1,128)S(1)}, f32[6,1,384]{2,1,0:T(1,128)S(1)}, u32[]{:S(2)}, u32[]{:S(2)}) collective-permute-start(f32[6,1,384]{2,1,0:T(1,128)S(1)} %pack_biases.1.bias), channel_id=1, source_target_pairs={{0,1},{1,0},{2,3},{3,2},{4,5},{5,4},{6,7},{7,6},{8,9},{9,8},{10,11... | collective-permute-start | bytes 27656 | tf_op jit(solution)/shard_map/ppermute | solution.py:522
  6.9 16.4 %collective-permute-start.7 = (bf16[768,384]{1,0:T(8,128)(2,1)}, bf16[768,384]{1,0:T(8,128)(2,1)}, u32[]{:S(2)}, u32[]{:S(2)}) collective-permute-start(bf16[768,384]{1,0:T(8,128)(2,1)} %pack_feed.1), channel_id=1, source_target_pairs={{0,1},{1,0},{2,3},{3,2},{4,5},{5,4},{6,7},{7,6},{8,9},{9,8},{10,11... | collective-permute-start | bytes 1769480 | tf_op jit(solution)/shard_map/ppermute | solution.py:522
  10.2 9.0 %collective-permute-start.2 = (bf16[4,96,384]{2,1,0:T(8,128)(2,1)S(1)}, bf16[4,96,384]{2,1,0:T(8,128)(2,1)S(1)}, u32[]{:S(2)}, u32[]{:S(2)}) collective-permute-start(bf16[4,96,384]{2,1,0:T(8,128)(2,1)S(1)} %collective-permute-done.n0), channel_id=1, source_target_pairs={{0,4},{2,6},{4,0},{6,2},{8,12},{10,14},{12,8},{14,10},{16,20},{18,... | collective-permute-start | bytes 884744 | tf_op jit(solution)/shard_map/ppermute | solution.py:519
  23.3 18.5 %collective-permute-start.11 = (bf16[768,384]{1,0:T(8,128)(2,1)}, bf16[768,384]{1,0:T(8,128)(2,1)S(1)}, u32[]{:S(2)}, u32[]{:S(2)}) collective-permute-start(bf16[768,384]{1,0:T(8,128)(2,1)} %collective-permute-done.7.f0), channel_id=1, source_target_pairs={{0,4},{2,6},{4,0},{6,2},{8,12},{10,14},{12,8},{14,10},{16,20},{18,... | collective-permute-start | bytes 1769480 | tf_op jit(solution)/shard_map/ppermute | solution.py:519
  24.4 17.5 %collective-permute-start.10 = (bf16[768,384]{1,0:T(8,128)(2,1)}, bf16[768,384]{1,0:T(8,128)(2,1)S(1)}, u32[]{:S(2)}, u32[]{:S(2)}) collective-permute-start(bf16[768,384]{1,0:T(8,128)(2,1)} %collective-permute-done.7.f0), channel_id=1, source_target_pairs={{0,8},{2,10},{4,12},{6,14},{8,0},{10,2},{12,4},{14,6},{16,24},{18,... | collective-permute-start | bytes 1769480 | tf_op jit(solution)/shard_map/ppermute | solution.py:519
  27.5 14.9 %collective-permute-start.12 = (bf16[768,384]{1,0:T(8,128)(2,1)S(1)}, bf16[768,384]{1,0:T(8,128)(2,1)S(1)}, u32[]{:S(2)}, u32[]{:S(2)}) collective-permute-start(bf16[768,384]{1,0:T(8,128)(2,1)S(1)} %pack_feed_d.1), channel_id=1, source_target_pairs={{0,1},{1,0},{2,3},{3,2},{4,5},{5,4},{6,7},{7,6},{8,9},{9,8},{10,11... | collective-permute-start | bytes 1769480 | tf_op jit(solution)/shard_map/ppermute | solution.py:522
  62.2 15.7 %collective-permute-start.19 = (bf16[2,2,2,96,768]{4,3,2,1,0:T(8,128)(2,1)S(1)}, bf16[2,2,2,96,768]{4,3,2,1,0:T(8,128)(2,1)S(1)}, u32[]{:S(2)}, u32[]{:S(2)}) collective-permute-start(bf16[2,2,2,96,768]{4,3,2,1,0:T(8,128)(2,1)S(1)} %add_half.9), channel_id=1, source_target_pairs={{0,1},{1,0},{2,10},{3,11},{4,5},{5,4},{6,14},{7,15},{8,9},{9,8},{1... | collective-permute-start | bytes 3538952 | tf_op jit(solution)/shard_map/ppermute | solution.py:530
  76.4 24.5 %collective-permute-start.22 = (bf16[2,2,2,192,384]{4,3,2,1,0:T(8,128)(2,1)S(1)}, bf16[2,2,2,192,384]{4,3,2,1,0:T(8,128)(2,1)S(1)}, u32[]{:S(2)}, u32[]{:S(2)}) collective-permute-start(bf16[2,2,2,192,384]{4,3,2,1,0:T(8,128)(2,1)S(1)} %add_half.10), channel_id=1, source_target_pairs={{0,1},{1,0},{2,10},{3,11},{4,5},{5,4},{6,14},{7,15},{8,9},{9,8},{1... | collective-permute-start | bytes 3538952 | tf_op jit(solution)/shard_map/ppermute | solution.py:530
  88.1 12.8 %collective-permute-start.20 = (bf16[2,2,96,768]{3,2,1,0:T(8,128)(2,1)S(1)}, bf16[2,2,96,768]{3,2,1,0:T(8,128)(2,1)S(1)}, u32[]{:S(2)}, u32[]{:S(2)}) collective-permute-start(bf16[2,2,96,768]{3,2,1,0:T(8,128)(2,1)S(1)} %add_half.11), channel_id=1, source_target_pairs={{0,4},{1,5},{2,3},{3,2},{4,0},{5,1},{6,7},{7,6},{8,12},{9,13},{10,... | collective-permute-start | bytes 1769480 | tf_op jit(solution)/shard_map/ppermute | solution.py:530
  92.7 19.6 %collective-permute-start.23 = (bf16[2,2,2,208,384]{4,3,2,1,0:T(8,128)(2,1)S(1)}, bf16[2,2,2,208,384]{4,3,2,1,0:T(8,128)(2,1)S(1)}, u32[]{:S(2)}, u32[]{:S(2)}) collective-permute-start(bf16[2,2,2,208,384]{4,3,2,1,0:T(8,128)(2,1)S(1)} %add_half.12), channel_id=1, source_target_pairs={{0,1},{1,0},{2,10},{3,11},{4,5},{5,4},{6,14},{7,15},{8,9},{9,8},{1... | collective-permute-start | bytes 3833864 | tf_op jit(solution)/shard_map/ppermute | solution.py:530
  106.6 12.1 %collective-permute-start.26 = (bf16[2,2,192,384]{3,2,1,0:T(8,128)(2,1)S(1)}, bf16[2,2,192,384]{3,2,1,0:T(8,128)(2,1)S(1)}, u32[]{:S(2)}, u32[]{:S(2)}) collective-permute-start(bf16[2,2,192,384]{3,2,1,0:T(8,128)(2,1)S(1)} %add_half.14), channel_id=1, source_target_pairs={{0,4},{1,5},{2,3},{3,2},{4,0},{5,1},{6,7},{7,6},{8,12},{9,13},{10,... | collective-permute-start | bytes 1769480 | tf_op jit(solution)/shard_map/ppermute | solution.py:530
  108.6 17.7 %collective-permute-start.29 = (bf16[2,96,768]{2,1,0:T(8,128)(2,1)S(1)}, bf16[2,96,768]{2,1,0:T(8,128)(2,1)S(1)}, u32[]{:S(2)}, u32[]{:S(2)}) collective-permute-start(bf16[2,96,768]{2,1,0:T(8,128)(2,1)S(1)} %add_all.3.refs_0_), channel_id=1, source_target_pairs={{0,16},{1,17},{2,18},{3,19},{4,20},{5,21},{6,22},{7,23},{8,24},{9,... | collective-permute-start | bytes 884744 | tf_op jit(solution)/shard_map/ppermute | solution.py:530
  113.1 12.4 %collective-permute-start.25 = (bf16[2,2,208,384]{3,2,1,0:T(8,128)(2,1)S(1)}, bf16[2,2,208,384]{3,2,1,0:T(8,128)(2,1)S(1)}, u32[]{:S(2)}, u32[]{:S(2)}) collective-permute-start(bf16[2,2,208,384]{3,2,1,0:T(8,128)(2,1)S(1)} %add_half.15), channel_id=1, source_target_pairs={{0,4},{1,5},{2,3},{3,2},{4,0},{5,1},{6,7},{7,6},{8,12},{9,13},{10,... | collective-permute-start | bytes 1916936 | tf_op jit(solution)/shard_map/ppermute | solution.py:530
  119.4 9.2 %collective-permute-start.28 = (bf16[2,192,384]{2,1,0:T(8,128)(2,1)S(1)}, bf16[2,192,384]{2,1,0:T(8,128)(2,1)S(1)}, u32[]{:S(2)}, u32[]{:S(2)}) collective-permute-start(bf16[2,192,384]{2,1,0:T(8,128)(2,1)S(1)} %add_half.16), channel_id=1, source_target_pairs={{0,8},{1,9},{2,6},{3,7},{4,12},{5,13},{6,2},{7,3},{8,0},{9,1},{10,... | collective-permute-start | bytes 884744 | tf_op jit(solution)/shard_map/ppermute | solution.py:530
  126.9 10.3 %collective-permute-start.31 = (bf16[2,96,768]{2,1,0:T(8,128)(2,1)S(1)}, bf16[2,96,768]{2,1,0:T(8,128)(2,1)S(1)}, u32[]{:S(2)}, u32[]{:S(2)}) collective-permute-start(bf16[2,96,768]{2,1,0:T(8,128)(2,1)S(1)} %add_two.3.a), channel_id=1, source_target_pairs={{0,8},{1,9},{2,6},{3,7},{4,12},{5,13},{6,2},{7,3},{8,0},{9,1},{10,... | collective-permute-start | bytes 884744 | tf_op jit(solution)/shard_map/ppermute | solution.py:530
  133.6 24.6 %collective-permute-start.30 = (bf16[2,208,384]{2,1,0:T(8,128)(2,1)S(1)}, bf16[2,208,384]{2,1,0:T(8,128)(2,1)S(1)}, u32[]{:S(2)}, u32[]{:S(2)}) collective-permute-start(bf16[2,208,384]{2,1,0:T(8,128)(2,1)S(1)} %add_all.5.refs_0_), channel_id=1, source_target_pairs={{0,16},{1,17},{2,18},{3,19},{4,20},{5,21},{6,22},{7,23},{8,24},{9,... | collective-permute-start | bytes 958472 | tf_op jit(solution)/shard_map/ppermute | solution.py:530
  137.9 22.8 %collective-permute-start.34 = (bf16[2,192,384]{2,1,0:T(8,128)(2,1)S(1)}, bf16[2,192,384]{2,1,0:T(8,128)(2,1)S(1)}, u32[]{:S(2)}, u32[]{:S(2)}) collective-permute-start(bf16[2,192,384]{2,1,0:T(8,128)(2,1)S(1)} %add_two.4.a), channel_id=1, source_target_pairs={{0,8},{1,9},{2,6},{3,7},{4,12},{5,13},{6,2},{7,3},{8,0},{9,1},{10,... | collective-permute-start | bytes 884744 | tf_op jit(solution)/shard_map/ppermute | solution.py:530
  139.8 25.8 %collective-permute-start.41 = (bf16[2,2,96,768]{3,2,1,0:T(8,128)(2,1)S(1)}, bf16[2,2,96,768]{3,2,1,0:T(8,128)(2,1)S(1)}, u32[]{:S(2)}, u32[]{:S(2)}) collective-permute-start(bf16[2,2,96,768]{3,2,1,0:T(8,128)(2,1)S(1)} %join.3.b0), channel_id=1, source_target_pairs={{0,4},{1,5},{2,10},{3,11},{4,0},{5,1},{6,14},{7,15},{8,12},{9,13},... | collective-permute-start | bytes 1769480 | tf_op jit(solution)/shard_map/ppermute | solution.py:530
  145.1 15.5 %collective-permute-start.35 = (bf16[2,2,96,768]{3,2,1,0:T(8,128)(2,1)S(1)}, bf16[2,2,96,768]{3,2,1,0:T(8,128)(2,1)S(1)}, u32[]{:S(2)}, u32[]{:S(2)}) collective-permute-start(bf16[2,2,96,768]{3,2,1,0:T(8,128)(2,1)S(1)} %join.3.b0), channel_id=1, source_target_pairs={{0,2},{2,0},{4,6},{6,4},{8,10},{10,8},{12,14},{14,12},{16,18},{18,... | collective-permute-start | bytes 1769480 | tf_op jit(solution)/shard_map/ppermute | solution.py:519
  158.9 12.6 %collective-permute-start.33 = (bf16[2,208,384]{2,1,0:T(8,128)(2,1)S(1)}, bf16[2,208,384]{2,1,0:T(8,128)(2,1)S(1)}, u32[]{:S(2)}, u32[]{:S(2)}) collective-permute-start(bf16[2,208,384]{2,1,0:T(8,128)(2,1)S(1)} %add_two.5.a), channel_id=1, source_target_pairs={{0,8},{1,9},{2,6},{3,7},{4,12},{5,13},{6,2},{7,3},{8,0},{9,1},{10,... | collective-permute-start | bytes 958472 | tf_op jit(solution)/shard_map/ppermute | solution.py:530
  161.3 11.9 %collective-permute-start.39 = (bf16[2,2,192,384]{3,2,1,0:T(8,128)(2,1)S(1)}, bf16[2,2,192,384]{3,2,1,0:T(8,128)(2,1)S(1)}, u32[]{:S(2)}, u32[]{:S(2)}) collective-permute-start(bf16[2,2,192,384]{3,2,1,0:T(8,128)(2,1)S(1)} %join.4.b0), channel_id=1, source_target_pairs={{0,4},{1,5},{2,10},{3,11},{4,0},{5,1},{6,14},{7,15},{8,12},{9,13},... | collective-permute-start | bytes 1769480 | tf_op jit(solution)/shard_map/ppermute | solution.py:530
  161.3 11.8 %collective-permute-start.38 = (bf16[2,2,192,384]{3,2,1,0:T(8,128)(2,1)S(1)}, bf16[2,2,192,384]{3,2,1,0:T(8,128)(2,1)S(1)}, u32[]{:S(2)}, u32[]{:S(2)}) collective-permute-start(bf16[2,2,192,384]{3,2,1,0:T(8,128)(2,1)S(1)} %join.4.b0), channel_id=1, source_target_pairs={{0,2},{2,0},{4,6},{6,4},{8,10},{10,8},{12,14},{14,12},{16,18},{18,... | collective-permute-start | bytes 1769480 | tf_op jit(solution)/shard_map/ppermute | solution.py:519
  172.1 12.1 %collective-permute-start.37 = (bf16[2,2,208,384]{3,2,1,0:T(8,128)(2,1)S(1)}, bf16[2,2,208,384]{3,2,1,0:T(8,128)(2,1)S(1)}, u32[]{:S(2)}, u32[]{:S(2)}) collective-permute-start(bf16[2,2,208,384]{3,2,1,0:T(8,128)(2,1)S(1)} %join.5.b0), channel_id=1, source_target_pairs={{0,4},{1,5},{2,10},{3,11},{4,0},{5,1},{6,14},{7,15},{8,12},{9,13},... | collective-permute-start | bytes 1916936 | tf_op jit(solution)/shard_map/ppermute | solution.py:530
  172.2 8.8 %collective-permute-start.36 = (bf16[2,2,208,384]{3,2,1,0:T(8,128)(2,1)S(1)}, bf16[2,2,208,384]{3,2,1,0:T(8,128)(2,1)S(1)}, u32[]{:S(2)}, u32[]{:S(2)}) collective-permute-start(bf16[2,2,208,384]{3,2,1,0:T(8,128)(2,1)S(1)} %join.5.b0), channel_id=1, source_target_pairs={{0,2},{2,0},{4,6},{6,4},{8,10},{10,8},{12,14},{14,12},{16,18},{18,... | collective-permute-start | bytes 1916936 | tf_op jit(solution)/shard_map/ppermute | solution.py:519
  (41 other events, 261.3 us)
